TPU v7x, 32 devices: a whole 2x2x4 slice. The times are simulated.
32 devices in a mesh: dp: 2 (over core), tm: 4 (over y, x), space: 4 (over z).
Axes of the slice: x: 2, y: 2, z: 4, core: 2. Of those that a mesh axis runs over, the one named last changes fastest.
Arguments:
- clip_latent: bfloat16 [2, 8, 64, 32, 256], P('dp', 'tm', 'space'), may hold values from -6 to 6
- grad_out: bfloat16 [2, 4, 64, 32, 256], P('dp', 'tm', 'space'), may hold values from -6 to 6
- w_spatial: bfloat16 [2304, 256], replicated, may hold values from -0.125 to 0.125
- w_temporal: bfloat16 [768, 256], replicated, may hold values from -0.21875 to 0.21875
- w_down: bfloat16 [768, 256], replicated, may hold values from -0.21875 to 0.21875
Outputs:
- latent_grad: bfloat16 [2, 8, 64, 32, 256], P('dp', 'tm', 'space')
- grad_spatial: float32 [256, 2304], P('space', ('dp', 'tm'))
- grad_temporal: float32 [256, 768], P('space', ('dp', 'tm'))
- grad_down: float32 [256, 768], P('space', ('dp', 'tm'))
All inputs are finite; a program needn't handle non-finite values.
Results may differ from a plain program's by a relative error of at most 0.0052.
Values may be sent and summed in bfloat16 or wider, within the bound.
A program may use at most 64 MiB of HBM per device.

v0:
```python
import math

import jax
import jax.numpy as jnp
from jax import lax
from jax.sharding import PartitionSpec as P


def padded_2(cells, sides, width):
    for axis, dim in sides:
        count = lax.axis_size(axis)
        ends = count - 1
        head = lax.slice_in_dim(cells, 0, width, axis=dim)
        tail = lax.slice_in_dim(cells, cells.shape[dim] - width, cells.shape[dim], axis=dim)
        cells = jnp.concatenate(
            [
                lax.ppermute(tail, axis, [(i, (i + 1) % count) for i in range(ends)]),
                cells,
                lax.ppermute(head, axis, [((i + 1) % count, i) for i in range(ends)]),
            ],
            axis=dim,
        )
    return cells


def from_behind(block, axis, distance):
    devices = range(lax.axis_size(axis))
    route = [(i - distance, i) for i in devices if i - distance in devices]
    return lax.ppermute(block, axis, route)


def merge_cells(values):
    return values.reshape(-1, values.shape[-1])


def pad_columns(values):
    return jnp.pad(values, ((0, 0), (0, 0), (0, 0), (1, 1), (0, 0)))


def spatial_columns(padded, rows, cols, flipped):
    pieces = []
    for i in range(3):
        for j in range(3):
            top = 2 - i if flipped else i
            left = 2 - j if flipped else j
            pieces.append(padded[:, :, top : top + rows, left : left + cols])
    return merge_cells(jnp.concatenate(pieces, axis=-1))


def frame_columns(extended, count, offsets):
    return merge_cells(jnp.concatenate([extended[:, o : o + count] for o in offsets], axis=-1))


def flip_blocks(weight, taps):
    chans = weight.shape[1]
    return weight.reshape(taps, chans, chans).transpose(0, 2, 1).reshape(taps * chans, chans)


def causal_mix(past, current, weight):
    extended = jnp.concatenate([past, current], axis=1)
    columns = frame_columns(extended, current.shape[1], (0, 1, 2))
    summed = jnp.dot(columns, weight, preferred_element_type=jnp.float32)
    return (columns, summed.reshape(current.shape))


def down_grad(extended_grad, count, flipped_down):
    shape = extended_grad.shape
    spread = jnp.stack([extended_grad, jnp.zeros_like(extended_grad)], axis=2)
    spread = spread.reshape((shape[0], 2 * shape[1]) + shape[2:])
    columns = frame_columns(spread, count, (2, 1, 0))
    summed = jnp.dot(columns, flipped_down, preferred_element_type=jnp.float32)
    return summed.reshape((shape[0], count) + shape[2:])


def per_device(clip_latent, grad_out, w_spatial, w_temporal, w_down):
    clips, frames, rows, cols, chans = clip_latent.shape
    half = grad_out.shape[1]
    total = (
        clips
        * frames
        * rows
        * cols
        * lax.axis_size("dp")
        * lax.axis_size("tm")
        * lax.axis_size("space")
    )
    scale = 1.0 / math.sqrt(total)
    rim_latent = padded_2(clip_latent, (("space", 2),), 1)
    columns_x = spatial_columns(pad_columns(rim_latent), rows, cols, False)
    pre_act = jnp.dot(columns_x, w_spatial, preferred_element_type=jnp.float32).reshape(
        clip_latent.shape
    )
    hidden = jax.nn.silu(pre_act).astype(jnp.bfloat16)
    past_hidden = from_behind(hidden, "tm", 1)
    columns_h, temporal_sum = causal_mix(past_hidden, hidden, w_temporal)
    mixed = (clip_latent.astype(jnp.float32) + temporal_sum).astype(jnp.bfloat16)
    past_mixed = from_behind(mixed, "tm", 1)
    flipped_down = flip_blocks(w_down, 3)
    flipped_temporal = flip_blocks(w_temporal, 3)
    flipped_spatial = flip_blocks(w_spatial, 9)
    next_grad = from_behind(grad_out, "tm", -1)
    own_wide = down_grad(jnp.concatenate([grad_out, next_grad], axis=1), frames, flipped_down)
    mixed_grad = own_wide.astype(jnp.bfloat16)
    next_mixed = from_behind(mixed_grad, "tm", -1)
    extended_dy = jnp.concatenate([mixed_grad, next_mixed], axis=1)
    columns_dy = frame_columns(extended_dy, frames, (2, 1, 0))
    hidden_grad = jnp.dot(columns_dy, flipped_temporal, preferred_element_type=jnp.float32).reshape(
        clip_latent.shape
    )
    sigma = jax.nn.sigmoid(pre_act)
    act_grad = (hidden_grad * sigma * (1.0 + pre_act * (1.0 - sigma))).astype(jnp.bfloat16)
    rim_grad = padded_2(act_grad, (("space", 2),), 1)
    columns_da = spatial_columns(pad_columns(rim_grad), rows, cols, True)
    spread_back = jnp.dot(columns_da, flipped_spatial, preferred_element_type=jnp.float32).reshape(
        clip_latent.shape
    )
    latent_grad = (mixed_grad.astype(jnp.float32) + spread_back).astype(jnp.bfloat16)
    act_cells = merge_cells(act_grad)
    dy_cells = merge_cells(mixed_grad)
    dz_cells = merge_cells(grad_out)
    extended_y = jnp.concatenate([past_mixed, mixed], axis=1)
    columns_y = merge_cells(
        jnp.concatenate([extended_y[:, k : k + 2 * half : 2] for k in range(3)], axis=-1)
    )

    def contract(left, right):
        term = lax.dot_general(
            left, right, (((0,), (0,)), ((), ())), preferred_element_type=jnp.float32
        )
        return scale * term

    local_terms = (
        contract(act_cells, columns_x),
        contract(dy_cells, columns_h),
        contract(dz_cells, columns_y),
    )
    core_parts = (
        lax.psum_scatter(local_terms[0], "dp", scatter_dimension=1, tiled=True),
        lax.psum_scatter(local_terms[1], "dp", scatter_dimension=1, tiled=True),
        lax.psum_scatter(local_terms[2], "dp", scatter_dimension=1, tiled=True),
    )
    band_parts = (
        lax.psum_scatter(core_parts[0], "space", scatter_dimension=0, tiled=True),
        lax.psum_scatter(core_parts[1], "space", scatter_dimension=0, tiled=True),
        lax.psum_scatter(core_parts[2], "space", scatter_dimension=0, tiled=True),
    )
    grad_spatial, grad_temporal, grad_down = (
        lax.psum_scatter(band_parts[0], "tm", scatter_dimension=1, tiled=True),
        lax.psum_scatter(band_parts[1], "tm", scatter_dimension=1, tiled=True),
        lax.psum_scatter(band_parts[2], "tm", scatter_dimension=1, tiled=True),
    )
    return (latent_grad, grad_spatial, grad_temporal, grad_down)


def solution(mesh):
    placed = (P("dp", "tm", "space", None, None), P("dp", "tm", "space", None, None), P(), P(), P())
    return jax.shard_map(
        per_device,
        mesh=mesh,
        in_specs=placed,
        out_specs=(
            P("dp", "tm", "space", None, None),
            P("space", ("dp", "tm")),
            P("space", ("dp", "tm")),
            P("space", ("dp", "tm")),
        ),
        check_vma=False,
    )
```

profile of v0, /device:TPU:0, one launch (start us, length us, event | category | flops | bytes accessed | tf_op | source)
XLA Modules:
  0.0 254.1 jit_solution(13539632051205830203)
XLA Ops:
  8.1 4.9 %collective-permute-start.2 = (bf16[1,2,1,32,256]{4,3,2,1,0:T(8,128)(2,1)S(1)}, bf16[1,2,1,32,256]{4,3,2,1,0:T(8,128)(2,1)S(1)}, u32[]{:S(2)}, u32[]{:S(2)}) collective-permute-start(bf16[1,2,1,32,256]{4,3,2,1,0:T(8,128)(2,1)S(1)} %get-tuple-element.19), channel_id=1, source_target_pairs={{0,1},{1,2},{2,3},{4,5},{5,6},{6,7},{8,9},{9,10},{10,11},{12,13},{... | collective-permute-start | bytes 98312 | tf_op jit(solution)/shard_map/ppermute | solution.py:17
  15.6 1.9 copy.15
  21.8 2.2 multiply_convert_fusion
  24.4 3.6 %collective-permute-start.6 = (bf16[1,2,16,32,256]{4,3,2,1,0:T(8,128)(2,1)S(1)}, bf16[1,2,16,32,256]{4,3,2,1,0:T(8,128)(2,1)S(1)}, u32[]{:S(2)}, u32[]{:S(2)}) collective-permute-start(bf16[1,2,16,32,256]{4,3,2,1,0:T(8,128)(2,1)S(1)} %multiply_convert_fusion.1), channel_id=1, source_target_pairs={{0,4},{4,8},{8,12},{1,5},{5,9},{9,13},{2,6},{6,10},{10,14},{3,7},{... | collective-permute-start | bytes 1572872 | tf_op jit(solution)/shard_map/ppermute | solution.py:29
  29.9 8.5 %collective-permute-done.6 = bf16[1,2,16,32,256]{4,3,2,1,0:T(8,128)(2,1)S(1)} collective-permute-done((bf16[1,2,16,32,256]{4,3,2,1,0:T(8,128)(2,1)S(1)}, bf16[1,2,16,32,256]{4,3,2,1,0:T(8,128)(2,1)S(1)}, u32[]{:S(2)}, u32[]{:S(2)}) %collective-permute-start.6) | collective-permute-done | bytes 524320 | tf_op jit(solution)/shard_map/ppermute | solution.py:29
  40.8 2.8 %fusion.38 = bf16[1,2,16,32,256]{4,3,2,1,0:T(8,128)(2,1)} fusion(bf16[1,2,16,32,256]{4,3,2,1,0:T(8,128)(2,1)} %bitcast.150, bf16[1,2,16,32,256]{4,3,2,1,0:T(8,128)(2,1)} %copy-done.4, bf16[1,2,16,32,256]{4,3,2,1,0:T(8,128)(2,1)} %copy-done.8, bf16[1,2,16,32,256]{4,3,2,1,0:T(8,128)(2,1)S(1)} %copy-done.1, bf16[768,256]{1,0:T(8,128)(2,1)} %param.8), kind=kOutput, calls=%fused_computation.34 | convolution fusion | flops 409731072 | bytes 3014656 | tf_op jit(solution)/shard_map/dot_general | solution.py:62
  43.6 5.2 %collective-permute-start.7 = (bf16[1,2,16,32,256]{4,3,2,1,0:T(8,128)(2,1)}, bf16[1,2,16,32,256]{4,3,2,1,0:T(8,128)(2,1)}, u32[]{:S(2)}, u32[]{:S(2)}) collective-permute-start(bf16[1,2,16,32,256]{4,3,2,1,0:T(8,128)(2,1)} %fusion.38), channel_id=1, source_target_pairs={{0,4},{4,8},{8,12},{1,5},{5,9},{9,13},{2,6},{6,10},{10,14},{3,7},{... | collective-permute-start | bytes 1572872 | tf_op jit(solution)/shard_map/ppermute | solution.py:29
  50.1 1.9 copy.16
  53.0 4.9 %collective-permute-done.7 = bf16[1,2,16,32,256]{4,3,2,1,0:T(8,128)(2,1)} collective-permute-done((bf16[1,2,16,32,256]{4,3,2,1,0:T(8,128)(2,1)}, bf16[1,2,16,32,256]{4,3,2,1,0:T(8,128)(2,1)}, u32[]{:S(2)}, u32[]{:S(2)}) %collective-permute-start.7) | collective-permute-done | bytes 524320 | tf_op jit(solution)/shard_map/ppermute | solution.py:29
  60.3 12.5 %collective-permute-done.1 = bf16[1,2,16,32,256]{4,3,2,1,0:T(8,128)(2,1)S(1)} collective-permute-done((bf16[1,2,16,32,256]{4,3,2,1,0:T(8,128)(2,1)S(1)}, bf16[1,2,16,32,256]{4,3,2,1,0:T(8,128)(2,1)S(1)}, u32[]{:S(2)}, u32[]{:S(2)}) %collective-permute-start.1) | collective-permute-done | bytes 524320 | tf_op jit(solution)/shard_map/ppermute | solution.py:29
  73.7 2.6 %fusion.40 = bf16[2,16,32,256]{3,2,1,0:T(8,128)(2,1)S(1)} fusion(bf16[768,256,1,1]{1,0,3,2:T(8,128)(2,1)} %bitcast.147, bf16[2,16,32,256]{3,2,1,0:T(8,128)(2,1)S(1)} %fusion.43, bf16[2,16,32,256]{3,2,1,0:T(8,128)(2,1)S(1)} %fusion.68, bf16[2,16,32,256]{3,2,1,0:T(8,128)(2,1)} %bitcast.143, f32[2,16,32,256]{3,2,1,0:T(8,128)S(1)} %bitcast.139), kind=kOutput, calls=%fused_computation.36 | convolution fusion | flops 409731072 | bytes 3538944 | tf_op jit(solution)/shard_map/dot_general | solution.py:107
  76.3 2.9 %fusion.7 = f32[256,2304]{1,0:T(8,128)} fusion(bf16[2,16,32,256]{3,2,1,0:T(8,128)(2,1)S(1)} %fusion.40, bf16[1,2,16,32,2304]{4,3,2,1,0:T(8,128)(2,1)S(1)} %bitcast.133), kind=kOutput, calls=%fused_computation.5 | convolution fusion | flops 1208549376 | bytes 7602176 | tf_op jit(solution)/shard_map/dot_general | solution.py:127
  79.8 1.9 copy.29
  81.8 7.8 %reduce-scatter.16.cloned.1.call-done = f32[256,1152]{1,0:T(8,128)} async-done(((f32[256,2304]{1,0:T(8,128)}), f32[256,1152]{1,0:T(8,128)}) %reduce-scatter.16.cloned.1.call-update) | async-done | bytes 1179664 | tf_op jit(solution)/shard_map/reduce_scatter | solution.py:138
  89.7 3.6 %collective-permute-start.4 = (bf16[1,2,1,32,256]{4,3,2,1,0:T(8,128)(2,1)S(1)}, bf16[1,2,1,32,256]{4,3,2,1,0:T(8,128)(2,1)S(1)}, u32[]{:S(2)}, u32[]{:S(2)}) collective-permute-start(bf16[1,2,1,32,256]{4,3,2,1,0:T(8,128)(2,1)S(1)} %get-tuple-element.17), channel_id=1, source_target_pairs={{0,1},{1,2},{2,3},{4,5},{5,6},{6,7},{8,9},{9,10},{10,11},{12,13},{... | collective-permute-start | bytes 98312 | tf_op jit(solution)/shard_map/ppermute | solution.py:17
  96.2 2.9 %collective-permute-done.5 = bf16[1,2,1,32,256]{4,3,2,1,0:T(8,128)(2,1)S(1)} collective-permute-done((bf16[1,2,1,32,256]{4,3,2,1,0:T(8,128)(2,1)S(1)}, bf16[1,2,1,32,256]{4,3,2,1,0:T(8,128)(2,1)S(1)}, u32[]{:S(2)}, u32[]{:S(2)}) %collective-permute-start.5) | collective-permute-done | bytes 32800 | tf_op jit(solution)/shard_map/ppermute | solution.py:19
  104.2 9.4 %reduce-scatter.22.cloned.1.call-done = f32[64,384]{1,0:T(8,128)} async-done(((f32[256,384]{1,0:T(8,128)}), f32[64,384]{1,0:T(8,128)}) %reduce-scatter.22.cloned.1.call-update) | async-done | bytes 98320 | tf_op jit(solution)/shard_map/reduce_scatter | solution.py:144
  116.3 18.9 %reduce-scatter.32.cloned.1.call-done = f32[64,384]{1,0:T(8,128)} async-done(((f32[256,384]{1,0:T(8,128)}), f32[64,384]{1,0:T(8,128)}) %reduce-scatter.32.cloned.1.call-update) | async-done | bytes 98320
  138.9 26.0 %reduce-scatter.18.cloned.1.call-done = f32[64,1152]{1,0:T(8,128)} async-done(((f32[256,1152]{1,0:T(8,128)}), f32[64,1152]{1,0:T(8,128)}) %reduce-scatter.18.cloned.1.call-update) | async-done | bytes 294928 | tf_op jit(solution)/shard_map/reduce_scatter | solution.py:143
  164.9 2.0 copy.25
  167.9 4.5 %fusion.50 = bf16[1,2,16,32,256]{4,3,2,1,0:T(8,128)(2,1)} fusion(bf16[2304,256,1,1]{1,0,3,2:T(8,128)(2,1)S(1)} %bitcast.137, bf16[1,2,16,32,2304]{4,3,2,1,0:T(8,128)(2,1)} %slice_dynamic-update-slice_fusion, bf16[2,16,32,256]{3,2,1,0:T(8,128)(2,1)S(1)} %fusion.43), kind=kOutput, calls=%fused_computation.43 | convolution fusion | flops 1208745984 | bytes 6946816 | tf_op jit(solution)/shard_map/dot_general | solution.py:114
  172.4 18.2 %reduce-scatter.30.cloned.1.call-done = f32[96,64]{1,0:T(8,128)} async-done(((f32[384,64]{1,0:T(8,128)}), f32[96,64]{1,0:T(8,128)}) %reduce-scatter.30.cloned.1.call-update) | async-done | bytes 24592
  192.1 25.5 %reduce-scatter.26.cloned.1.call-done = f32[64,96]{0,1:T(8,128)} async-done(((f32[64,384]{0,1:T(8,128)}), f32[64,96]{0,1:T(8,128)}) %reduce-scatter.26.cloned.1.call-update) | async-done | bytes 24592 | tf_op jit(solution)/shard_map/reduce_scatter | solution.py:150
  219.1 26.7 %reduce-scatter.28.cloned.1.call-done = f32[288,64]{1,0:T(8,128)} async-done(((f32[1152,64]{1,0:T(8,128)}), f32[288,64]{1,0:T(8,128)}) %reduce-scatter.28.cloned.1.call-update) | async-done | bytes 73744
  (89 shorter events, 38.3 us)
Async XLA Ops:
  7.2 13.1 %copy-start.1 = (bf16[1,2,16,32,256]{4,3,2,1,0:T(8,128)(2,1)S(1)}, bf16[1,2,16,32,256]{4,3,2,1,0:T(8,128)(2,1)}, u32[]{:S(2)}) copy-start(bf16[1,2,16,32,256]{4,3,2,1,0:T(8,128)(2,1)} %param.5) | copy-start | bytes 1572868
  7.2 72.1 %reduce-scatter.20.cloned.1.call-start = ((), (), s32[]{:S(2)}) async-start(), calls=%async_computation.11 | async-start | bytes 1179648 | tf_op jit(solution)/shard_map/reduce_scatter | solution.py:139
  8.1 9.5 %collective-permute-start.2 = (bf16[1,2,1,32,256]{4,3,2,1,0:T(8,128)(2,1)S(1)}, bf16[1,2,1,32,256]{4,3,2,1,0:T(8,128)(2,1)S(1)}, u32[]{:S(2)}, u32[]{:S(2)}) collective-permute-start(bf16[1,2,1,32,256]{4,3,2,1,0:T(8,128)(2,1)S(1)} %get-tuple-element.19), channel_id=1, source_target_pairs={{0,1},{1,2},{2,3},{4,5},{5,6},{6,7},{8,9},{9,10},{10,11},{12,13},{... | collective-permute-start | bytes 98312 | tf_op jit(solution)/shard_map/ppermute | solution.py:17
  13.0 5.8 %collective-permute-start.3 = (bf16[1,2,1,32,256]{4,3,2,1,0:T(8,128)(2,1)S(1)}, bf16[1,2,1,32,256]{4,3,2,1,0:T(8,128)(2,1)S(1)}, u32[]{:S(2)}, u32[]{:S(2)}) collective-permute-start(bf16[1,2,1,32,256]{4,3,2,1,0:T(8,128)(2,1)S(1)} %get-tuple-element.20), channel_id=1, source_target_pairs={{1,0},{2,1},{3,2},{5,4},{6,5},{7,6},{9,8},{10,9},{11,10},{13,12},{... | collective-permute-start | bytes 98312 | tf_op jit(solution)/shard_map/ppermute | solution.py:19
  14.3 13.6 %collective-permute-start = (bf16[1,1,16,32,256]{4,3,2,1,0:T(8,128)(2,1)}, bf16[1,1,16,32,256]{4,3,2,1,0:T(8,128)(2,1)}, u32[]{:S(2)}, u32[]{:S(2)}) collective-permute-start(bf16[1,1,16,32,256]{4,3,2,1,0:T(8,128)(2,1)} %param.6), channel_id=1, source_target_pairs={{4,0},{8,4},{12,8},{5,1},{9,5},{13,9},{6,2},{10,6},{14,10},{7,3},{... | collective-permute-start | bytes 786440 | tf_op jit(solution)/shard_map/ppermute | solution.py:29
  21.2 2.8 %copy-start = (bf16[1,2,16,32,2304]{4,3,2,1,0:T(8,128)(2,1)}, bf16[1,2,16,32,2304]{4,3,2,1,0:T(8,128)(2,1)S(1)}, u32[]{:S(2)}) copy-start(bf16[1,2,16,32,2304]{4,3,2,1,0:T(8,128)(2,1)S(1)} %slice_dynamic-update-slice_fusion.6) | copy-start | bytes 14155780
  21.8 6.1 %copy-start.7 = (bf16[1,1,16,32,256]{4,3,2,1,0:T(8,128)(2,1)S(1)}, bf16[1,1,16,32,256]{4,3,2,1,0:T(8,128)(2,1)}, u32[]{:S(2)}) copy-start(bf16[1,1,16,32,256]{4,3,2,1,0:T(8,128)(2,1)} %param.6) | copy-start | bytes 786436
  24.3 14.0 %copy-start.4 = (bf16[1,2,16,32,256]{4,3,2,1,0:T(8,128)(2,1)}, bf16[1,2,16,32,256]{4,3,2,1,0:T(8,128)(2,1)S(1)}, u32[]{:S(2)}) copy-start(bf16[1,2,16,32,256]{4,3,2,1,0:T(8,128)(2,1)S(1)} %multiply_convert_fusion.1) | copy-start | bytes 1572868
  24.3 4.9 %copy-start.6 = (bf16[3,256,256]{2,1,0:T(8,128)(2,1)S(1)}, bf16[3,256,256]{2,1,0:T(8,128)(2,1)}, u32[]{:S(2)}) copy-start(bf16[3,256,256]{2,1,0:T(8,128)(2,1)} %copy.15) | copy-start | bytes 1179652
  24.4 14.0 %collective-permute-start.6 = (bf16[1,2,16,32,256]{4,3,2,1,0:T(8,128)(2,1)S(1)}, bf16[1,2,16,32,256]{4,3,2,1,0:T(8,128)(2,1)S(1)}, u32[]{:S(2)}, u32[]{:S(2)}) collective-permute-start(bf16[1,2,16,32,256]{4,3,2,1,0:T(8,128)(2,1)S(1)} %multiply_convert_fusion.1), channel_id=1, source_target_pairs={{0,4},{4,8},{8,12},{1,5},{5,9},{9,13},{2,6},{6,10},{10,14},{3,7},{... | collective-permute-start | bytes 1572872 | tf_op jit(solution)/shard_map/ppermute | solution.py:29
  40.7 39.1 %reduce-scatter.24.cloned.1.call-start = ((), (), s32[]{:S(2)}) async-start(), calls=%async_computation.13 | async-start | bytes 1179648 | tf_op jit(solution)/shard_map/reduce_scatter | solution.py:140
  43.6 14.3 %collective-permute-start.7 = (bf16[1,2,16,32,256]{4,3,2,1,0:T(8,128)(2,1)}, bf16[1,2,16,32,256]{4,3,2,1,0:T(8,128)(2,1)}, u32[]{:S(2)}, u32[]{:S(2)}) collective-permute-start(bf16[1,2,16,32,256]{4,3,2,1,0:T(8,128)(2,1)} %fusion.38), channel_id=1, source_target_pairs={{0,4},{4,8},{8,12},{1,5},{5,9},{9,13},{2,6},{6,10},{10,14},{3,7},{... | collective-permute-start | bytes 1572872 | tf_op jit(solution)/shard_map/ppermute | solution.py:29
  48.8 24.1 %collective-permute-start.1 = (bf16[1,2,16,32,256]{4,3,2,1,0:T(8,128)(2,1)S(1)}, bf16[1,2,16,32,256]{4,3,2,1,0:T(8,128)(2,1)S(1)}, u32[]{:S(2)}, u32[]{:S(2)}) collective-permute-start(bf16[1,2,16,32,256]{4,3,2,1,0:T(8,128)(2,1)S(1)} %bitcast.141), channel_id=1, source_target_pairs={{4,0},{8,4},{12,8},{5,1},{9,5},{13,9},{6,2},{10,6},{14,10},{7,3},{... | collective-permute-start | bytes 1572872 | tf_op jit(solution)/shard_map/ppermute | solution.py:29
  60.3 29.3 %reduce-scatter.16.cloned.1.call-start = ((), (), s32[]{:S(2)}) async-start(), calls=%async_computation.9 | async-start | bytes 3538944 | tf_op jit(solution)/shard_map/reduce_scatter | solution.py:138
  72.9 3.4 %slice-start = ((s8[4718592]{0:T(1024)(128)(4,1)}), s8[4194304]{0:T(1024)(128)(4,1)S(1)}, s32[]{:S(2)}) async-start(s8[4718592]{0:T(1024)(128)(4,1)} %bitcast.132), calls=%async_computation.18 | async-start | bytes 8388608
  79.2 34.4 %reduce-scatter.22.cloned.1.call-start = ((), (), s32[]{:S(2)}) async-start(), calls=%async_computation.12 | async-start | bytes 491520 | tf_op jit(solution)/shard_map/reduce_scatter | solution.py:144
  79.8 55.4 %reduce-scatter.32.cloned.1.call-start = ((), (), s32[]{:S(2)}) async-start(), calls=%async_computation.17 | async-start | bytes 491520
  81.8 83.2 %reduce-scatter.18.cloned.1.call-start = ((), (), s32[]{:S(2)}) async-start(), calls=%async_computation.10 | async-start | bytes 1474560 | tf_op jit(solution)/shard_map/reduce_scatter | solution.py:143
  89.6 101.0 %reduce-scatter.30.cloned.1.call-start = ((), (), s32[]{:S(2)}) async-start(), calls=%async_computation.16 | async-start | bytes 245760
  89.7 6.5 %collective-permute-start.4 = (bf16[1,2,1,32,256]{4,3,2,1,0:T(8,128)(2,1)S(1)}, bf16[1,2,1,32,256]{4,3,2,1,0:T(8,128)(2,1)S(1)}, u32[]{:S(2)}, u32[]{:S(2)}) collective-permute-start(bf16[1,2,1,32,256]{4,3,2,1,0:T(8,128)(2,1)S(1)} %get-tuple-element.17), channel_id=1, source_target_pairs={{0,1},{1,2},{2,3},{4,5},{5,6},{6,7},{8,9},{9,10},{10,11},{12,13},{... | collective-permute-start | bytes 98312 | tf_op jit(solution)/shard_map/ppermute | solution.py:17
  93.3 5.8 %collective-permute-start.5 = (bf16[1,2,1,32,256]{4,3,2,1,0:T(8,128)(2,1)S(1)}, bf16[1,2,1,32,256]{4,3,2,1,0:T(8,128)(2,1)S(1)}, u32[]{:S(2)}, u32[]{:S(2)}) collective-permute-start(bf16[1,2,1,32,256]{4,3,2,1,0:T(8,128)(2,1)S(1)} %get-tuple-element.18), channel_id=1, source_target_pairs={{1,0},{2,1},{3,2},{5,4},{6,5},{7,6},{9,8},{10,9},{11,10},{13,12},{... | collective-permute-start | bytes 98312 | tf_op jit(solution)/shard_map/ppermute | solution.py:19
  115.3 52.6 %copy-start.3 = (bf16[9,256,256]{2,1,0:T(8,128)(2,1)S(1)}, bf16[9,256,256]{2,1,0:T(8,128)(2,1)}, u32[]{:S(2)}) copy-start(bf16[9,256,256]{2,1,0:T(8,128)(2,1)} %copy.17) | copy-start | bytes 3538948
  115.3 102.3 %reduce-scatter.26.cloned.1.call-start = ((), (), s32[]{:S(2)}) async-start(), calls=%async_computation.14 | async-start | bytes 245760 | tf_op jit(solution)/shard_map/reduce_scatter | solution.py:150
  136.9 108.9 %reduce-scatter.28.cloned.1.call-start = ((), (), s32[]{:S(2)}) async-start(), calls=%async_computation.15 | async-start | bytes 737280
  (4 other events, 5.5 us)
Sparse Core Ops, SparseCore 0:
  40.8 12.1 reduce-scatter.19
  60.4 15.8 reduce-scatter.23
  79.3 10.2 reduce-scatter.15
  91.8 21.7 reduce-scatter.21
  116.3 18.8 reduce-scatter.31
  137.5 27.4 reduce-scatter.17
  167.9 22.7 reduce-scatter.29
  193.6 23.9 reduce-scatter.25
  220.7 25.0 reduce-scatter.27
where the time goes:
time: 255 us; the launch traced here: 254 us
  waiting for transfers between devices  163 us (64%)
  local copies, waits for them, and re-layouts  30.4 us (12%)
  starting transfers between devices  22.8 us (9%)
  matrix products  18.4 us (7%)
  between operations  14.2 us (6%)
  other arithmetic  4.94 us (2%)
    unnamed x12, waiting for transfers between devices  64.5 us
    reduce_scatter x1, waiting for transfers between devices, per_device(): lax.psum_scatter(core_parts[0], 'space', scatter_dimension=0, tiled=True)  26 us
    ppermute x4, waiting for transfers between devices, from_behind(): return lax.ppermute(block, axis, route)  25.9 us
    reduce_scatter x1, waiting for transfers between devices, per_device(): lax.psum_scatter(band_parts[2], 'tm', scatter_dimension=1, tiled=True)  25.5 us
    unnamed x41, local copies, waits for them, and re-layouts  20.6 us
    ppermute x4, starting transfers between devices, from_behind(): return lax.ppermute(block, axis, route)  11.3 us
    reduce_scatter x1, waiting for transfers between devices, per_device(): lax.psum_scatter(core_parts[1], 'space', scatter_dimension=0, tiled=True)  9.42 us
    ppermute x2, starting transfers between devices, padded_2(): lax.ppermute(tail, axis, [(i, (i + 1) % count) for i in range(ends)])  8.54 us
  transfers between devices with their start and end apart: 17, of which 12 were waited for; matrix products, arithmetic and copies ran while one was open for 19% of the time, Pallas kernels for 0%

commit v1 on v0

v1 whole, which is shorter than its diff:
```python
import functools
import math

import jax
import jax.numpy as jnp
from jax import lax
from jax.experimental import pallas as pl
from jax.experimental.pallas import tpu as pltpu
from jax.sharding import PartitionSpec as P


def padded_2(cells, sides, width):
    for axis, dim in sides:
        count = lax.axis_size(axis)
        ends = count - 1
        head = lax.slice_in_dim(cells, 0, width, axis=dim)
        tail = lax.slice_in_dim(cells, cells.shape[dim] - width, cells.shape[dim], axis=dim)
        cells = jnp.concatenate(
            [
                lax.ppermute(tail, axis, [(i, (i + 1) % count) for i in range(ends)]),
                cells,
                lax.ppermute(head, axis, [((i + 1) % count, i) for i in range(ends)]),
            ],
            axis=dim,
        )
    return cells


def from_behind(block, axis, distance):
    devices = range(lax.axis_size(axis))
    route = [(i - distance, i) for i in devices if i - distance in devices]
    return lax.ppermute(block, axis, route)


def merge_cells(values):
    return values.reshape(-1, values.shape[-1])


def pad_columns(values):
    return jnp.pad(values, ((0, 0), (0, 0), (0, 0), (1, 1), (0, 0)))


def spatial_columns(padded, rows, cols, flipped):
    pieces = []
    for i in range(3):
        for j in range(3):
            top = 2 - i if flipped else i
            left = 2 - j if flipped else j
            pieces.append(padded[:, :, top : top + rows, left : left + cols])
    return merge_cells(jnp.concatenate(pieces, axis=-1))


def frame_columns(extended, count, offsets):
    return merge_cells(jnp.concatenate([extended[:, o : o + count] for o in offsets], axis=-1))


def flip_blocks(weight, taps):
    chans = weight.shape[1]
    return weight.reshape(taps, chans, chans).transpose(0, 2, 1).reshape(taps * chans, chans)


def causal_mix(past, current, weight):
    extended = jnp.concatenate([past, current], axis=1)
    columns = frame_columns(extended, current.shape[1], (0, 1, 2))
    summed = jnp.dot(columns, weight, preferred_element_type=jnp.float32)
    return summed.reshape(current.shape)


def round_up(size, step):
    return (size + step - 1) // step * step


def reduce_kernel(
    groups,
    bands,
    scale,
    parts_ref,
    out_ref,
    from_core,
    mid,
    from_group,
    total,
    turned,
    turned_wide,
    from_band,
    core_send,
    core_recv,
    group_send,
    group_recv,
    band_send,
    band_recv,
):
    core = lax.axis_index("dp")
    group = lax.axis_index("tm")
    band = lax.axis_index("space")
    rows = parts_ref.shape[2]
    chans = parts_ref.shape[3]

    def at(d, t, s):
        return dict(device_id=(d, t, s), device_id_type=pl.DeviceIdType.MESH)

    barrier = pltpu.get_barrier_semaphore()
    pl.semaphore_signal(barrier, inc=1, **at(1 - core, group, band))
    for i in range(groups - 1):
        pl.semaphore_signal(barrier, inc=1, **at(core, lax.rem(group + 1 + i, groups), band))
    for i in range(bands - 1):
        pl.semaphore_signal(barrier, inc=1, **at(core, group, lax.rem(band + 1 + i, bands)))
    pl.semaphore_wait(barrier, groups + bands - 1)

    core_copies = []
    for i in range(groups):
        target = lax.rem(group + 1 + i, groups)
        copy = pltpu.make_async_remote_copy(
            src_ref=parts_ref.at[1 - core, target],
            dst_ref=from_core.at[i],
            send_sem=core_send.at[i],
            recv_sem=core_recv.at[i],
            **at(1 - core, group, band),
        )
        copy.start()
        core_copies.append(copy)

    group_copies = []
    for i in range(groups):
        target = lax.rem(group + 1 + i, groups)
        core_copies[i].wait_recv()
        summed = parts_ref[core, target].astype(jnp.float32) + from_core[i].astype(jnp.float32)
        if i == groups - 1:
            total[0:rows, :] = summed
        else:
            mid[i] = summed.astype(jnp.bfloat16)
            copy = pltpu.make_async_remote_copy(
                src_ref=mid.at[i],
                dst_ref=from_group.at[i],
                send_sem=group_send.at[i],
                recv_sem=group_recv.at[i],
                **at(core, target, band),
            )
            copy.start()
            group_copies.append(copy)
    if total.shape[0] > rows:
        total[rows:, :] = jnp.zeros((total.shape[0] - rows, chans), jnp.float32)
    for i in range(groups - 1):
        group_copies[i].wait_recv()
        total[0:rows, :] += from_group[i].astype(jnp.float32)

    flat = (total[...] * scale).T.reshape(turned.shape)
    turned_wide[...] = flat
    turned[...] = flat.astype(jnp.bfloat16)
    band_copies = []
    for i in range(bands - 1):
        target = lax.rem(band + 1 + i, bands)
        copy = pltpu.make_async_remote_copy(
            src_ref=turned.at[target],
            dst_ref=from_band.at[i],
            send_sem=band_send.at[i],
            recv_sem=band_recv.at[i],
            **at(core, group, target),
        )
        copy.start()
        band_copies.append(copy)
    result = turned_wide[band]
    for i in range(bands - 1):
        band_copies[i].wait_recv()
        result += from_band[i].astype(jnp.float32)
    out_ref[...] = result
    for copy in core_copies + group_copies + band_copies:
        copy.wait_send()


def reduce_parts(parts, scale):
    cores, groups, rows, chans = parts.shape
    bands = lax.axis_size("space")
    wide = round_up(rows, 128)
    share = chans // bands
    dma = pltpu.SemaphoreType.DMA
    return pl.pallas_call(
        functools.partial(reduce_kernel, groups, bands, scale),
        out_shape=jax.ShapeDtypeStruct((share, wide), jnp.float32),
        in_specs=[pl.BlockSpec(memory_space=pltpu.VMEM)],
        out_specs=pl.BlockSpec(memory_space=pltpu.VMEM),
        scratch_shapes=[
            pltpu.VMEM((groups, rows, chans), jnp.bfloat16),
            pltpu.VMEM((groups - 1, rows, chans), jnp.bfloat16),
            pltpu.VMEM((groups - 1, rows, chans), jnp.bfloat16),
            pltpu.VMEM((wide, chans), jnp.float32),
            pltpu.VMEM((bands, share, wide), jnp.bfloat16),
            pltpu.VMEM((bands, share, wide), jnp.float32),
            pltpu.VMEM((bands - 1, share, wide), jnp.bfloat16),
            dma((groups,)),
            dma((groups,)),
            dma((groups - 1,)),
            dma((groups - 1,)),
            dma((bands - 1,)),
            dma((bands - 1,)),
        ],
        compiler_params=pltpu.CompilerParams(
            collective_id=0, has_side_effects=True, vmem_limit_bytes=40 * 1024 * 1024
        ),
    )(parts)


def per_device(clip_latent, grad_out, w_spatial, w_temporal, w_down):
    clips, frames, rows, cols, chans = clip_latent.shape
    assert frames == 2 and grad_out.shape[1] == 1
    groups = lax.axis_size("tm")
    cores = lax.axis_size("dp")
    total = clips * frames * rows * cols * cores * groups * lax.axis_size("space")
    scale = 1.0 / math.sqrt(total)
    rim_latent = padded_2(clip_latent, (("space", 2),), 1)
    next_grad = from_behind(grad_out, "tm", -1)
    later_grad = from_behind(grad_out, "tm", -2)
    columns_x = spatial_columns(pad_columns(rim_latent), rows, cols, False)
    pre_act = jnp.dot(columns_x, w_spatial, preferred_element_type=jnp.float32).reshape(
        clip_latent.shape
    )
    hidden = jax.nn.silu(pre_act).astype(jnp.bfloat16)
    past_hidden = from_behind(hidden, "tm", 1)

    down = w_down.reshape(3, chans, chans)
    flipped_temporal = flip_blocks(w_temporal, 3)
    flipped_spatial = flip_blocks(w_spatial, 9)
    ahead_grad = jnp.concatenate([grad_out, next_grad, later_grad], axis=1)
    even_weight = jnp.concatenate([down[2], down[0]], axis=1)
    even_columns = jnp.concatenate([ahead_grad[:, 0:2], ahead_grad[:, 1:3]], axis=-1)

    def times_transpose(left, weight):
        return lax.dot_general(
            left, weight, (((4,), (1,)), ((), ())), preferred_element_type=jnp.float32
        ).astype(jnp.bfloat16)

    even = times_transpose(even_columns, even_weight)
    odd = times_transpose(ahead_grad[:, 1:3], down[1])
    extended_dy = jnp.concatenate([even[:, 0:1], odd[:, 0:1], even[:, 1:2], odd[:, 1:2]], axis=1)
    mixed_grad = extended_dy[:, 0:2]
    columns_dy = frame_columns(extended_dy, frames, (2, 1, 0))
    hidden_grad = jnp.dot(columns_dy, flipped_temporal, preferred_element_type=jnp.float32).reshape(
        clip_latent.shape
    )
    sigma = jax.nn.sigmoid(pre_act)
    act_grad = (hidden_grad * sigma * (1.0 + pre_act * (1.0 - sigma))).astype(jnp.bfloat16)
    rim_grad = padded_2(act_grad, (("space", 2),), 1)

    temporal_sum = causal_mix(past_hidden, hidden, w_temporal)
    mixed = (clip_latent.astype(jnp.float32) + temporal_sum).astype(jnp.bfloat16)

    def contract(left, right):
        return lax.dot_general(
            merge_cells(left),
            merge_cells(right),
            (((0,), (0,)), ((), ())),
            preferred_element_type=jnp.float32,
        ).astype(jnp.bfloat16)

    spatial_part = contract(columns_x, act_grad)
    temporal_part = jnp.concatenate(
        [contract(hidden, extended_dy[:, 2 - k : 4 - k]) for k in range(3)], axis=0
    )
    down_part = jnp.concatenate(
        [
            contract(mixed[:, 0:1], next_grad),
            contract(mixed[:, 1:2], next_grad),
            contract(mixed[:, 0:1], grad_out),
        ],
        axis=0,
    )
    pieces = [
        part.reshape(cores, groups, -1, chans) for part in (spatial_part, temporal_part, down_part)
    ]
    sizes = [piece.shape[2] for piece in pieces]
    fill = -sum(sizes) % 16
    if fill:
        pieces.append(jnp.zeros((cores, groups, fill, chans), jnp.bfloat16))
    reduced = reduce_parts(jnp.concatenate(pieces, axis=2), scale)
    grad_spatial = reduced[:, : sizes[0]]
    grad_temporal = reduced[:, sizes[0] : sizes[0] + sizes[1]]
    grad_down = reduced[:, sizes[0] + sizes[1] : sum(sizes)]

    columns_da = spatial_columns(pad_columns(rim_grad), rows, cols, True)
    spread_back = jnp.dot(columns_da, flipped_spatial, preferred_element_type=jnp.float32).reshape(
        clip_latent.shape
    )
    latent_grad = (mixed_grad.astype(jnp.float32) + spread_back).astype(jnp.bfloat16)
    return (latent_grad, grad_spatial, grad_temporal, grad_down)


def solution(mesh):
    placed = (P("dp", "tm", "space", None, None), P("dp", "tm", "space", None, None), P(), P(), P())
    return jax.shard_map(
        per_device,
        mesh=mesh,
        in_specs=placed,
        out_specs=(
            P("dp", "tm", "space", None, None),
            P("space", ("dp", "tm")),
            P("space", ("dp", "tm")),
            P("space", ("dp", "tm")),
        ),
        check_vma=False,
    )
```

time: 255 us -> 69.2 us (0.27)
  waiting for transfers between devices: 163 us -> 5.24 us
  Pallas kernels: 0 us -> 24.1 us
  local copies, waits for them, and re-layouts: 30.4 us -> 8.32 us
  between operations: 14.2 us -> 1.05 us
  matrix products: 18.4 us -> 10 us
  starting transfers between devices: 22.8 us -> 18.6 us
  other arithmetic: 4.94 us -> 1.36 us
    reduce_scatter x6 -> x0, waiting for transfers between devices: 68.7 us -> none  [the longest x1 26 us: per_device(): lax.psum_scatter(core_parts[0], 'space', scatter_dimension=0, tiled=True)]
    unnamed x12 -> x0, waiting for transfers between devices: 64.5 us -> none
    ppermute x4 -> x3, waiting for transfers between devices: 25.9 us -> 0.01 us  [from_behind(): return lax.ppermute(block, axis, route)]
    pallas_call x0 -> x1, Pallas kernels: none -> 24.1 us  [reduce_parts(): pl.pallas_call(functools.partial(reduce_kernel, groups, bands, scale), ou...]
    unnamed x41 -> x21, local copies, waits for them, and re-layouts: 20.6 us -> 2.03 us
    ppermute x4 -> x3, starting transfers between devices: 11.3 us -> 7.3 us  [from_behind(): return lax.ppermute(block, axis, route)]
    transpose x3 -> x2, local copies, waits for them, and re-layouts: 5.44 us -> 2.74 us  [flip_blocks(): weight.reshape(taps, chans, chans).transpose(0, 2, 1)]
    unnamed x6 -> x4, other arithmetic: 2.82 us -> 0.15 us
  transfers between devices with their start and end apart: 17 -> 7, of which waited for: 12 -> 3; matrix products, arithmetic and copies ran while one was open for 19% -> 24% of each run, Pallas kernels for 0% -> 0%
where the time goes in v1:
time: 69.2 us; the launch traced here: 68.7 us
  Pallas kernels  24.1 us (35%)
  starting transfers between devices  18.6 us (27%)
  matrix products  10 us (14%)
  local copies, waits for them, and re-layouts  8.32 us (12%)
  waiting for transfers between devices  5.24 us (8%)
  other arithmetic  1.36 us (2%)
  between operations  1.05 us (2%)
    pallas_call x1, Pallas kernels, reduce_parts(): pl.pallas_call(functools.partial(reduce_kernel, groups, bands, scale), ou...  24.1 us
    ppermute x2, starting transfers between devices, padded_2(): lax.ppermute(tail, axis, [(i, (i + 1) % count) for i in range(ends)])  8.74 us
    ppermute x3, starting transfers between devices, from_behind(): return lax.ppermute(block, axis, route)  7.3 us
    ppermute x2, waiting for transfers between devices, padded_2(): lax.ppermute(head, axis, [((i + 1) % count, i) for i in range(ends)])  4.99 us
    dot_general x7, matrix products, contract(): lax.dot_general(merge_cells(left), merge_cells(right), (((0,), (0,)), (()...  3.3 us
    transpose x2, local copies, waits for them, and re-layouts, flip_blocks(): weight.reshape(taps, chans, chans).transpose(0, 2, 1)  2.74 us
    ppermute x2, starting transfers between devices, padded_2(): lax.ppermute(head, axis, [((i + 1) % count, i) for i in range(ends)])  2.58 us
    dot_general x1, matrix products, per_device(): jnp.dot(columns_da, flipped_spatial, preferred_element_type=jnp.float32)  2.19 us
  transfers between devices with their start and end apart: 7, of which 3 were waited for; matrix products, arithmetic and copies ran while one was open for 24% of the time, Pallas kernels for 0%

profile of v1, /device:TPU:0, one launch (start us, length us, event | category | flops | bytes accessed | tf_op | source)
XLA Modules:
  0.0 68.7 jit_solution(6243036559449261491)
XLA Ops:
  0.6 1.4 %collective-permute-start = (bf16[1,1,16,32,256]{4,3,2,1,0:T(8,128)(2,1)}, bf16[1,1,16,32,256]{4,3,2,1,0:T(8,128)(2,1)S(1)}, u32[]{:S(2)}, u32[]{:S(2)}) collective-permute-start(bf16[1,1,16,32,256]{4,3,2,1,0:T(8,128)(2,1)} %param.6), channel_id=1, source_target_pairs={{4,0},{8,4},{12,8},{5,1},{9,5},{13,9},{6,2},{10,6},{14,10},{7,3},{... | collective-permute-start | bytes 786440 | tf_op jit(solution)/shard_map/ppermute | solution.py:32
  2.1 1.3 %collective-permute-start.1 = (bf16[1,1,16,32,256]{4,3,2,1,0:T(8,128)(2,1)}, bf16[1,1,16,32,256]{4,3,2,1,0:T(8,128)(2,1)S(1)}, u32[]{:S(2)}, u32[]{:S(2)}) collective-permute-start(bf16[1,1,16,32,256]{4,3,2,1,0:T(8,128)(2,1)} %param.6), channel_id=1, source_target_pairs={{8,0},{12,4},{9,1},{13,5},{10,2},{14,6},{11,3},{15,7},{24,16},{28,... | collective-permute-start | bytes 786440 | tf_op jit(solution)/shard_map/ppermute | solution.py:32
  3.4 0.8 %fusion.94 = (bf16[1,2,1,32,256]{4,3,2,1,0:T(8,128)(2,1)S(1)}, bf16[1,2,1,32,256]{4,3,2,1,0:T(8,128)(2,1)S(1)}) fusion(bf16[1,2,16,32,256]{4,3,2,1,0:T(8,128)(2,1)} %param.5), kind=kLoop, calls=%fused_computation.125 | loop fusion | bytes 131072 | tf_op jit(solution)/shard_map/slice | solution.py:17
  4.2 4.9 %collective-permute-start.2 = (bf16[1,2,1,32,256]{4,3,2,1,0:T(8,128)(2,1)S(1)}, bf16[1,2,1,32,256]{4,3,2,1,0:T(8,128)(2,1)S(1)}, u32[]{:S(2)}, u32[]{:S(2)}) collective-permute-start(bf16[1,2,1,32,256]{4,3,2,1,0:T(8,128)(2,1)S(1)} %get-tuple-element.12), channel_id=1, source_target_pairs={{0,1},{1,2},{2,3},{4,5},{5,6},{6,7},{8,9},{9,10},{10,11},{12,13},{... | collective-permute-start | bytes 98312 | tf_op jit(solution)/shard_map/ppermute | solution.py:20
  9.1 1.3 %collective-permute-start.3 = (bf16[1,2,1,32,256]{4,3,2,1,0:T(8,128)(2,1)S(1)}, bf16[1,2,1,32,256]{4,3,2,1,0:T(8,128)(2,1)S(1)}, u32[]{:S(2)}, u32[]{:S(2)}) collective-permute-start(bf16[1,2,1,32,256]{4,3,2,1,0:T(8,128)(2,1)S(1)} %get-tuple-element.13), channel_id=1, source_target_pairs={{1,0},{2,1},{3,2},{5,4},{6,5},{7,6},{9,8},{10,9},{11,10},{13,12},{... | collective-permute-start | bytes 98312 | tf_op jit(solution)/shard_map/ppermute | solution.py:22
  10.4 1.0 %fusion.95 = (bf16[256,256]{1,0:T(8,128)(2,1)S(1)}, bf16[256,256]{1,0:T(8,128)(2,1)S(1)}) fusion(bf16[768,256]{1,0:T(8,128)(2,1)} %param.9), kind=kLoop, calls=%fused_computation.126 | loop fusion | bytes 524288 | tf_op jit(solution)/shard_map/slice | solution.py:224
  11.4 1.2 %copy.9 = bf16[3,256,256]{2,1,0:T(8,128)(2,1)S(1)} copy(bf16[3,256,256]{1,2,0:T(8,128)(2,1)} %bitcast.176) | data formatting | bytes 786432 | tf_op jit(solution)/shard_map/transpose | solution.py:59
  12.5 1.6 %copy.10 = bf16[9,256,256]{2,1,0:T(8,128)(2,1)S(1)} copy(bf16[9,256,256]{1,2,0:T(8,128)(2,1)} %bitcast.171) | data formatting | bytes 2359296 | tf_op jit(solution)/shard_map/transpose | solution.py:59
  14.1 0.8 %collective-permute-done.3 = bf16[1,2,1,32,256]{4,3,2,1,0:T(8,128)(2,1)S(1)} collective-permute-done((bf16[1,2,1,32,256]{4,3,2,1,0:T(8,128)(2,1)S(1)}, bf16[1,2,1,32,256]{4,3,2,1,0:T(8,128)(2,1)S(1)}, u32[]{:S(2)}, u32[]{:S(2)}) %collective-permute-start.3) | collective-permute-done | bytes 32800 | tf_op jit(solution)/shard_map/ppermute | solution.py:22
  16.3 0.6 copy-done.1
  16.9 1.4 %multiply_convert_fusion.1 = (bf16[1024,256]{1,0:T(8,128)(2,1)S(1)}, f32[1024,256]{1,0:T(8,128)S(1)}) fusion(bf16[1024,2304]{1,0:T(8,128)(2,1)S(1)} %bitcast.178, bf16[2304,256]{1,0:T(8,128)(2,1)S(1)} %copy-done.1), kind=kOutput, calls=%fused_computation.61 | convolution fusion | flops 1209270272 | bytes 7471104 | tf_op jit(solution)/shard_map/dot_general | solution.py:214
  18.6 4.6 %collective-permute-start.6 = (bf16[1,2,16,32,256]{4,3,2,1,0:T(8,128)(2,1)S(1)}, bf16[1,2,16,32,256]{4,3,2,1,0:T(8,128)(2,1)S(1)}, u32[]{:S(2)}, u32[]{:S(2)}) collective-permute-start(bf16[1,2,16,32,256]{4,3,2,1,0:T(8,128)(2,1)S(1)} %multiply_convert_fusion), channel_id=1, source_target_pairs={{0,4},{4,8},{8,12},{1,5},{5,9},{9,13},{2,6},{6,10},{10,14},{3,7},{... | collective-permute-start | bytes 1572872 | tf_op jit(solution)/shard_map/ppermute | solution.py:32
  23.3 1.2 %fusion.52 = bf16[1,2,16,32,256]{4,3,2,1,0:T(8,128)(2,1)S(1)} fusion(bf16[1,2,16,32,256]{4,3,2,1,0:T(8,128)(2,1)S(1)} %constant_dynamic-update-slice_fusion, bf16[768,256]{1,0:T(8,128)(2,1)} %param.9), kind=kOutput, calls=%fused_computation.42 | convolution fusion | flops 134479872 | bytes 1179648 | tf_op jit(solution)/shard_map/dot_general | solution.py:228
  24.5 0.5 fusion.51
  26.2 0.8 %fusion.41 = bf16[2,16,32,256]{3,2,1,0:T(8,128)(2,1)S(1)} fusion(bf16[768,256,1,1]{1,0,3,2:T(8,128)(2,1)S(1)} %bitcast.177, bf16[1,1,16,32,256]{4,3,2,1,0:T(8,128)(2,1)S(1)} %get-tuple-element.9, bf16[1,1,16,32,256]{4,3,2,1,0:T(8,128)(2,1)S(1)} %get-tuple-element.20, bf16[1,1,16,32,256]{4,3,2,1,0:T(8,128)(2,1)S(1)} %get-tuple-element.21, ...), kind=kOutput, calls=%fused_computation.35 | convolution fusion | flops 414449664 | bytes 3014656 | tf_op jit(solution)/shard_map/dot_general | solution.py:237
  27.0 1.4 %fusion.7 = bf16[2304,256]{1,0:T(8,128)(2,1)S(1)} fusion(bf16[2,16,32,256]{3,2,1,0:T(8,128)(2,1)S(1)} %fusion.41, bf16[1,2,16,32,2304]{4,3,2,1,0:T(8,128)(2,1)S(1)} %slice_dynamic-update-slice_fusion.6), kind=kOutput, calls=%fused_computation.5 | convolution fusion | flops 1208549376 | bytes 6422528 | tf_op jit(solution)/shard_map/dot_general | solution.py:248
  28.5 3.8 %collective-permute-start.4 = (bf16[1,2,1,32,256]{4,3,2,1,0:T(8,128)(2,1)S(1)}, bf16[1,2,1,32,256]{4,3,2,1,0:T(8,128)(2,1)S(1)}, u32[]{:S(2)}, u32[]{:S(2)}) collective-permute-start(bf16[1,2,1,32,256]{4,3,2,1,0:T(8,128)(2,1)S(1)} %get-tuple-element.10), channel_id=1, source_target_pairs={{0,1},{1,2},{2,3},{4,5},{5,6},{6,7},{8,9},{9,10},{10,11},{12,13},{... | collective-permute-start | bytes 98312 | tf_op jit(solution)/shard_map/ppermute | solution.py:20
  32.3 1.3 %collective-permute-start.5 = (bf16[1,2,1,32,256]{4,3,2,1,0:T(8,128)(2,1)S(1)}, bf16[1,2,1,32,256]{4,3,2,1,0:T(8,128)(2,1)S(1)}, u32[]{:S(2)}, u32[]{:S(2)}) collective-permute-start(bf16[1,2,1,32,256]{4,3,2,1,0:T(8,128)(2,1)S(1)} %get-tuple-element.11), channel_id=1, source_target_pairs={{1,0},{2,1},{3,2},{5,4},{6,5},{7,6},{9,8},{10,9},{11,10},{13,12},{... | collective-permute-start | bytes 98312 | tf_op jit(solution)/shard_map/ppermute | solution.py:22
  33.9 4.2 %collective-permute-done.5 = bf16[1,2,1,32,256]{4,3,2,1,0:T(8,128)(2,1)S(1)} collective-permute-done((bf16[1,2,1,32,256]{4,3,2,1,0:T(8,128)(2,1)S(1)}, bf16[1,2,1,32,256]{4,3,2,1,0:T(8,128)(2,1)S(1)}, u32[]{:S(2)}, u32[]{:S(2)}) %collective-permute-start.5) | collective-permute-done | bytes 32800 | tf_op jit(solution)/shard_map/ppermute | solution.py:22
  39.5 2.2 %fusion.48 = bf16[1,2,16,32,256]{4,3,2,1,0:T(8,128)(2,1)} fusion(bf16[2304,256,1,1]{1,0,3,2:T(8,128)(2,1)S(1)} %bitcast.172, bf16[1,2,16,32,2304]{4,3,2,1,0:T(8,128)(2,1)S(1)} %slice_dynamic-update-slice_fusion, bf16[1,16,32,256]{3,2,1,0:T(8,128)(2,1)S(1)} %get-tuple-element.7, bf16[1,16,32,256]{3,2,1,0:T(8,128)(2,1)S(1)} %get-tuple-element.22), kind=kOutput, calls=%fused_computation.40 | convolution fusion | flops 1209008128 | bytes 6946816 | tf_op jit(solution)/shard_map/dot_general | solution.py:280
  41.7 0.6 fusion.42
  43.3 24.1 %shard_map.84 = f32[64,512]{1,0:T(8,128)S(1)} custom-call(bf16[2,4,480,256]{3,2,1,0:T(8,128)(2,1)S(1)} %pad_maximum_fusion.parts_ref), custom_call_target="tpu_custom_call" | custom-call | tf_op jit(solution)/shard_map/pallas_call | solution.py:177
  67.3 0.6 slice.160
  68.0 0.7 %fusion.96 = (f32[64,96]{1,0:T(8,128)}, f32[64,96]{1,0:T(8,128)}) fusion(f32[64,512]{1,0:T(8,128)S(1)} %shard_map.84), kind=kLoop, calls=%fused_computation.127 | loop fusion | bytes 98304 | tf_op jit(solution)/shard_map/slice | solution.py:277
  (46 shorter events, 5.4 us)
Async XLA Ops:
  0.6 14.3 %copy-start = (bf16[1,2,16,32,256]{4,3,2,1,0:T(8,128)(2,1)S(1)}, bf16[1,2,16,32,256]{4,3,2,1,0:T(8,128)(2,1)}, u32[]{:S(2)}) copy-start(bf16[1,2,16,32,256]{4,3,2,1,0:T(8,128)(2,1)} %param.5) | copy-start | bytes 1572868
  0.6 22.6 %collective-permute-start = (bf16[1,1,16,32,256]{4,3,2,1,0:T(8,128)(2,1)}, bf16[1,1,16,32,256]{4,3,2,1,0:T(8,128)(2,1)S(1)}, u32[]{:S(2)}, u32[]{:S(2)}) collective-permute-start(bf16[1,1,16,32,256]{4,3,2,1,0:T(8,128)(2,1)} %param.6), channel_id=1, source_target_pairs={{4,0},{8,4},{12,8},{5,1},{9,5},{13,9},{6,2},{10,6},{14,10},{7,3},{... | collective-permute-start | bytes 786440 | tf_op jit(solution)/shard_map/ppermute | solution.py:32
  2.1 21.2 %collective-permute-start.1 = (bf16[1,1,16,32,256]{4,3,2,1,0:T(8,128)(2,1)}, bf16[1,1,16,32,256]{4,3,2,1,0:T(8,128)(2,1)S(1)}, u32[]{:S(2)}, u32[]{:S(2)}) collective-permute-start(bf16[1,1,16,32,256]{4,3,2,1,0:T(8,128)(2,1)} %param.6), channel_id=1, source_target_pairs={{8,0},{12,4},{9,1},{13,5},{10,2},{14,6},{11,3},{15,7},{24,16},{28,... | collective-permute-start | bytes 786440 | tf_op jit(solution)/shard_map/ppermute | solution.py:32
  4.2 10.0 %collective-permute-start.2 = (bf16[1,2,1,32,256]{4,3,2,1,0:T(8,128)(2,1)S(1)}, bf16[1,2,1,32,256]{4,3,2,1,0:T(8,128)(2,1)S(1)}, u32[]{:S(2)}, u32[]{:S(2)}) collective-permute-start(bf16[1,2,1,32,256]{4,3,2,1,0:T(8,128)(2,1)S(1)} %get-tuple-element.12), channel_id=1, source_target_pairs={{0,1},{1,2},{2,3},{4,5},{5,6},{6,7},{8,9},{9,10},{10,11},{12,13},{... | collective-permute-start | bytes 98312 | tf_op jit(solution)/shard_map/ppermute | solution.py:20
  9.1 5.8 %collective-permute-start.3 = (bf16[1,2,1,32,256]{4,3,2,1,0:T(8,128)(2,1)S(1)}, bf16[1,2,1,32,256]{4,3,2,1,0:T(8,128)(2,1)S(1)}, u32[]{:S(2)}, u32[]{:S(2)}) collective-permute-start(bf16[1,2,1,32,256]{4,3,2,1,0:T(8,128)(2,1)S(1)} %get-tuple-element.13), channel_id=1, source_target_pairs={{1,0},{2,1},{3,2},{5,4},{6,5},{7,6},{9,8},{10,9},{11,10},{13,12},{... | collective-permute-start | bytes 98312 | tf_op jit(solution)/shard_map/ppermute | solution.py:22
  15.6 1.3 %copy-start.1 = (bf16[2304,256]{1,0:T(8,128)(2,1)S(1)}, bf16[2304,256]{1,0:T(8,128)(2,1)}, u32[]{:S(2)}) copy-start(bf16[2304,256]{1,0:T(8,128)(2,1)} %param.7) | copy-start | bytes 3538948
  18.3 6.2 %copy-start.3 = (bf16[1,1,16,32,256]{4,3,2,1,0:T(8,128)(2,1)S(1)}, bf16[1,1,16,32,256]{4,3,2,1,0:T(8,128)(2,1)}, u32[]{:S(2)}) copy-start(bf16[1,1,16,32,256]{4,3,2,1,0:T(8,128)(2,1)} %param.6) | copy-start | bytes 786436
  18.6 23.1 %collective-permute-start.6 = (bf16[1,2,16,32,256]{4,3,2,1,0:T(8,128)(2,1)S(1)}, bf16[1,2,16,32,256]{4,3,2,1,0:T(8,128)(2,1)S(1)}, u32[]{:S(2)}, u32[]{:S(2)}) collective-permute-start(bf16[1,2,16,32,256]{4,3,2,1,0:T(8,128)(2,1)S(1)} %multiply_convert_fusion), channel_id=1, source_target_pairs={{0,4},{4,8},{8,12},{1,5},{5,9},{9,13},{2,6},{6,10},{10,14},{3,7},{... | collective-permute-start | bytes 1572872 | tf_op jit(solution)/shard_map/ppermute | solution.py:32
  28.5 5.4 %collective-permute-start.4 = (bf16[1,2,1,32,256]{4,3,2,1,0:T(8,128)(2,1)S(1)}, bf16[1,2,1,32,256]{4,3,2,1,0:T(8,128)(2,1)S(1)}, u32[]{:S(2)}, u32[]{:S(2)}) collective-permute-start(bf16[1,2,1,32,256]{4,3,2,1,0:T(8,128)(2,1)S(1)} %get-tuple-element.10), channel_id=1, source_target_pairs={{0,1},{1,2},{2,3},{4,5},{5,6},{6,7},{8,9},{9,10},{10,11},{12,13},{... | collective-permute-start | bytes 98312 | tf_op jit(solution)/shard_map/ppermute | solution.py:20
  32.3 5.8 %collective-permute-start.5 = (bf16[1,2,1,32,256]{4,3,2,1,0:T(8,128)(2,1)S(1)}, bf16[1,2,1,32,256]{4,3,2,1,0:T(8,128)(2,1)S(1)}, u32[]{:S(2)}, u32[]{:S(2)}) collective-permute-start(bf16[1,2,1,32,256]{4,3,2,1,0:T(8,128)(2,1)S(1)} %get-tuple-element.11), channel_id=1, source_target_pairs={{1,0},{2,1},{3,2},{5,4},{6,5},{7,6},{9,8},{10,9},{11,10},{13,12},{... | collective-permute-start | bytes 98312 | tf_op jit(solution)/shard_map/ppermute | solution.py:22
  39.5 2.2 %copy-start.2 = (bf16[768,256]{1,0:T(8,128)(2,1)S(1)}, bf16[768,256]{1,0:T(8,128)(2,1)}, u32[]{:S(2)}) copy-start(bf16[768,256]{1,0:T(8,128)(2,1)} %param.8) | copy-start | bytes 1179652

commit v2 on v1

v2 whole, which is shorter than its diff:
```python
import functools
import math

import jax
import jax.numpy as jnp
from jax import lax
from jax.experimental import pallas as pl
from jax.experimental.pallas import tpu as pltpu
from jax.sharding import PartitionSpec as P

F32 = jnp.float32
BF16 = jnp.bfloat16


def round_up(size, step):
    return (size + step - 1) // step * step


def dot_nn(left, right):
    return jnp.dot(left, right, preferred_element_type=F32)


def dot_nt(left, right):
    return lax.dot_general(left, right, (((1,), (1,)), ((), ())), preferred_element_type=F32)


def dot_tn(left, right):
    return lax.dot_general(left, right, (((0,), (0,)), ((), ())), preferred_element_type=F32)


def block_kernel(
    groups,
    bands,
    cols,
    scale,
    x_ref,
    go_ref,
    ws_ref,
    wt_ref,
    wd_ref,
    latent_ref,
    out_ref,
    x_pad,
    x_shift,
    a_pad,
    a_shift,
    pre,
    hid,
    ahead,
    dy,
    parts,
    outgoing,
    from_core,
    mid,
    from_group,
    total,
    turned,
    turned_wide,
    from_band,
    edge_send,
    edge_recv,
    core_send,
    core_recv,
    group_send,
    group_recv,
    band_send,
    band_recv,
):
    core = lax.axis_index("dp")
    group = lax.axis_index("tm")
    band = lax.axis_index("space")
    chans = x_ref.shape[2]
    cells = x_ref.shape[1]
    rows = parts.shape[2]
    share = (9 * chans // (2 * groups), 3 * chans // (2 * groups), 3 * chans // (2 * groups))
    first = (0, share[0], share[0] + share[1])

    def at(d, t, s):
        return dict(device_id=(d, t, s), device_id_type=pl.DeviceIdType.MESH)

    barrier = pltpu.get_barrier_semaphore()
    pl.semaphore_signal(barrier, inc=1, **at(1 - core, group, band))
    for i in range(groups - 1):
        pl.semaphore_signal(barrier, inc=1, **at(core, lax.rem(group + 1 + i, groups), band))
    for i in range(bands - 1):
        pl.semaphore_signal(barrier, inc=1, **at(core, group, lax.rem(band + 1 + i, bands)))
    pl.semaphore_wait(barrier, groups + bands - 1)

    def make(n, src, dst, where):
        return pltpu.make_async_remote_copy(
            src_ref=src,
            dst_ref=dst,
            send_sem=edge_send.at[n],
            recv_sem=edge_recv.at[n],
            **where,
        )

    below = lax.rem(band + 1, bands)
    above = lax.rem(band + bands - 1, bands)
    before = lax.rem(group + groups - 1, groups)
    before2 = lax.rem(group + groups - 2, groups)
    after = lax.rem(group + 1, groups)
    low = pl.ds(0, cols)
    high = pl.ds(cells + cols, cols)
    moves = (
        (
            lambda: make(0, x_ref.at[:, pl.ds(cells - cols, cols)], x_pad.at[:, low], at(core, group, below)),
            band < bands - 1,
            band > 0,
        ),
        (
            lambda: make(1, x_ref.at[:, pl.ds(0, cols)], x_pad.at[:, high], at(core, group, above)),
            band > 0,
            band < bands - 1,
        ),
        (
            lambda: make(2, go_ref, ahead.at[0], at(core, before, band)),
            group > 0,
            group < groups - 1,
        ),
        (
            lambda: make(3, go_ref, ahead.at[1], at(core, before2, band)),
            group > 1,
            group < groups - 2,
        ),
        (
            lambda: make(4, hid.at[pl.ds(2, 2)], hid.at[pl.ds(0, 2)], at(core, after, band)),
            group < groups - 1,
            group > 0,
        ),
        (
            lambda: make(5, a_pad.at[:, pl.ds(cells, cols)], a_pad.at[:, low], at(core, group, below)),
            band < bands - 1,
            band > 0,
        ),
        (
            lambda: make(6, a_pad.at[:, pl.ds(cols, cols)], a_pad.at[:, high], at(core, group, above)),
            band > 0,
            band < bands - 1,
        ),
    )

    def start(n):
        @pl.when(moves[n][1])
        def _():
            moves[n][0]().start()

    def arrive(n):
        @pl.when(moves[n][2])
        def _():
            moves[n][0]().wait_recv()

    def sent(n):
        @pl.when(moves[n][1])
        def _():
            moves[n][0]().wait_send()

    for n in range(4):
        start(n)

    edge_zero = jnp.zeros((2, cols, chans), BF16)

    @pl.when(band == 0)
    def _():
        x_pad[:, 0:cols] = edge_zero
        a_pad[:, 0:cols] = edge_zero

    @pl.when(band == bands - 1)
    def _():
        x_pad[:, cells + cols : cells + 2 * cols] = edge_zero
        a_pad[:, cells + cols : cells + 2 * cols] = edge_zero

    @pl.when(group == groups - 1)
    def _():
        ahead[0] = jnp.zeros((cells, chans), BF16)

    @pl.when(group >= groups - 2)
    def _():
        ahead[1] = jnp.zeros((cells, chans), BF16)

    @pl.when(group == 0)
    def _():
        hid[0:2] = jnp.zeros((2, cells, chans), BF16)

    def shift(source, target, order):
        length = cells + 2 * cols
        place = lax.rem(lax.broadcasted_iota(jnp.int32, (length, chans), 0), cols)
        for f in range(2):
            plain = source[f]
            wide = plain.astype(F32)
            left = jnp.where(place == 0, 0.0, pltpu.roll(wide, 1, 0)).astype(BF16)
            right = jnp.where(place == cols - 1, 0.0, pltpu.roll(wide, length - 1, 0)).astype(BF16)
            values = (left, plain, right)
            for j in range(3):
                target[f, :, j * chans : (j + 1) * chans] = values[order[j]]

    x_pad[:, cols : cells + cols] = x_ref[...]
    arrive(0)
    arrive(1)
    shift(x_pad, x_shift, (0, 1, 2))
    for f in range(2):
        acc = jnp.zeros((cells, chans), F32)
        for i in range(3):
            acc += dot_nn(
                x_shift[f, i * cols : i * cols + cells, :],
                ws_ref[3 * i * chans : 3 * (i + 1) * chans, :],
            )
        pre[f] = acc
        hid[2 + f] = (acc / (1.0 + jnp.exp(-acc))).astype(BF16)
    start(4)

    arrive(2)
    arrive(3)

    def down(k):
        return wd_ref[k * chans : (k + 1) * chans, :]

    def temporal(k):
        return wt_ref[k * chans : (k + 1) * chans, :]

    dy[0] = (dot_nt(go_ref[...], down(2)) + dot_nt(ahead[0], down(0))).astype(BF16)
    dy[1] = dot_nt(ahead[0], down(1)).astype(BF16)
    dy[2] = (dot_nt(ahead[0], down(2)) + dot_nt(ahead[1], down(0))).astype(BF16)
    dy[3] = dot_nt(ahead[1], down(1)).astype(BF16)
    for f in range(2):
        back = jnp.zeros((cells, chans), F32)
        for k in range(3):
            back += dot_nt(dy[f + 2 - k], temporal(k))
        value = pre[f]
        gate = 1.0 / (1.0 + jnp.exp(-value))
        a_pad[f, cols : cells + cols] = (back * gate * (1.0 + value * (1.0 - gate))).astype(BF16)
    start(5)
    start(6)

    def put(kind, begin, values):
        done = 0
        size = values.shape[0]
        while done < size:
            spot = begin + done
            owner, inner = spot // share[kind], spot % share[kind]
            count = min(share[kind] - inner, size - done)
            offset = first[kind] + inner
            parts[owner // groups, owner % groups, offset : offset + count, :] = values[
                done : done + count
            ]
            done += count

    if rows > sum(share):
        for d in range(2):
            for t in range(groups):
                parts[d, t, sum(share) :, :] = jnp.zeros((rows - sum(share), chans), F32)

    for i in range(3):
        for j in range(3):
            acc = jnp.zeros((chans, chans), F32)
            for f in range(2):
                acc += dot_tn(
                    x_shift[f, i * cols : i * cols + cells, j * chans : (j + 1) * chans],
                    a_pad[f, cols : cells + cols, :],
                )
            put(0, (3 * i + j) * chans, acc)
    for k in range(3):
        put(1, k * chans, dot_tn(hid[2], dy[2 - k]) + dot_tn(hid[3], dy[3 - k]))

    arrive(4)
    mixed = []
    for f in range(2):
        acc = x_ref[f].astype(F32)
        acc += (
            dot_nn(hid[f], temporal(0))
            + dot_nn(hid[f + 1], temporal(1))
            + dot_nn(hid[f + 2], temporal(2))
        )
        mixed.append(acc.astype(BF16))
    put(2, 0, dot_tn(mixed[0], ahead[0]))
    put(2, chans, dot_tn(mixed[1], ahead[0]))
    put(2, 2 * chans, dot_tn(mixed[0], go_ref[...]))

    core_copies = []
    for i in range(groups):
        target = lax.rem(group + 1 + i, groups)
        outgoing[i] = parts[1 - core, target].astype(BF16)
        copy = pltpu.make_async_remote_copy(
            src_ref=outgoing.at[i],
            dst_ref=from_core.at[i],
            send_sem=core_send.at[i],
            recv_sem=core_recv.at[i],
            **at(1 - core, group, band),
        )
        copy.start()
        core_copies.append(copy)

    group_copies = []
    for i in range(groups):
        target = lax.rem(group + 1 + i, groups)
        core_copies[i].wait_recv()
        summed = parts[core, target] + from_core[i].astype(F32)
        if i == groups - 1:
            total[0:rows, :] = summed
        else:
            mid[i] = summed.astype(BF16)
            copy = pltpu.make_async_remote_copy(
                src_ref=mid.at[i],
                dst_ref=from_group.at[i],
                send_sem=group_send.at[i],
                recv_sem=group_recv.at[i],
                **at(core, target, band),
            )
            copy.start()
            group_copies.append(copy)
    if total.shape[0] > rows:
        total[rows:, :] = jnp.zeros((total.shape[0] - rows, chans), F32)

    arrive(5)
    arrive(6)
    shift(a_pad, a_shift, (2, 1, 0))
    for f in range(2):
        acc = dy[f].astype(F32)
        for i in range(3):
            for j in range(3):
                tap = 3 * i + j
                acc += dot_nt(
                    a_shift[f, (2 - i) * cols : (2 - i) * cols + cells, j * chans : (j + 1) * chans],
                    ws_ref[tap * chans : (tap + 1) * chans, :],
                )
        latent_ref[f] = acc.astype(BF16)

    for i in range(groups - 1):
        group_copies[i].wait_recv()
        total[0:rows, :] += from_group[i].astype(F32)

    flat = (total[...] * scale).T.reshape(turned.shape)
    turned_wide[...] = flat
    turned[...] = flat.astype(BF16)
    band_copies = []
    for i in range(bands - 1):
        target = lax.rem(band + 1 + i, bands)
        copy = pltpu.make_async_remote_copy(
            src_ref=turned.at[target],
            dst_ref=from_band.at[i],
            send_sem=band_send.at[i],
            recv_sem=band_recv.at[i],
            **at(core, group, target),
        )
        copy.start()
        band_copies.append(copy)
    result = turned_wide[band]
    for i in range(bands - 1):
        band_copies[i].wait_recv()
        result += from_band[i].astype(F32)
    out_ref[...] = result
    for n in range(7):
        sent(n)
    for copy in core_copies + group_copies + band_copies:
        copy.wait_send()


def per_device(clip_latent, grad_out, w_spatial, w_temporal, w_down):
    clips, frames, height, cols, chans = clip_latent.shape
    groups = lax.axis_size("tm")
    bands = lax.axis_size("space")
    assert clips == 1 and frames == 2 and grad_out.shape[1] == 1 and lax.axis_size("dp") == 2
    count = clips * frames * height * cols * 2 * groups * bands
    scale = 1.0 / math.sqrt(count)
    cells = height * cols
    padded = cells + 2 * cols
    sizes = (9 * chans // (2 * groups), 3 * chans // (2 * groups), 3 * chans // (2 * groups))
    rows = round_up(sum(sizes), 16)
    wide = round_up(rows, 128)
    share = chans // bands
    dma = pltpu.SemaphoreType.DMA
    vmem = pl.BlockSpec(memory_space=pltpu.VMEM)
    latent, reduced = pl.pallas_call(
        functools.partial(block_kernel, groups, bands, cols, scale),
        out_shape=(
            jax.ShapeDtypeStruct((2, cells, chans), BF16),
            jax.ShapeDtypeStruct((share, wide), F32),
        ),
        in_specs=[vmem] * 5,
        out_specs=(vmem, vmem),
        scratch_shapes=[
            pltpu.VMEM((2, padded, chans), BF16),
            pltpu.VMEM((2, padded, 3 * chans), BF16),
            pltpu.VMEM((2, padded, chans), BF16),
            pltpu.VMEM((2, padded, 3 * chans), BF16),
            pltpu.VMEM((2, cells, chans), F32),
            pltpu.VMEM((4, cells, chans), BF16),
            pltpu.VMEM((2, cells, chans), BF16),
            pltpu.VMEM((4, cells, chans), BF16),
            pltpu.VMEM((2, groups, rows, chans), F32),
            pltpu.VMEM((groups, rows, chans), BF16),
            pltpu.VMEM((groups, rows, chans), BF16),
            pltpu.VMEM((groups - 1, rows, chans), BF16),
            pltpu.VMEM((groups - 1, rows, chans), BF16),
            pltpu.VMEM((wide, chans), F32),
            pltpu.VMEM((bands, share, wide), BF16),
            pltpu.VMEM((bands, share, wide), F32),
            pltpu.VMEM((bands - 1, share, wide), BF16),
            dma((7,)),
            dma((7,)),
            dma((groups,)),
            dma((groups,)),
            dma((groups - 1,)),
            dma((groups - 1,)),
            dma((bands - 1,)),
            dma((bands - 1,)),
        ],
        compiler_params=pltpu.CompilerParams(
            collective_id=0, has_side_effects=True, vmem_limit_bytes=50 * 1024 * 1024
        ),
    )(
        clip_latent.reshape(2, cells, chans),
        grad_out.reshape(cells, chans),
        w_spatial,
        w_temporal,
        w_down,
    )
    return (
        latent.reshape(clip_latent.shape),
        reduced[:, : sizes[0]],
        reduced[:, sizes[0] : sizes[0] + sizes[1]],
        reduced[:, sizes[0] + sizes[1] : sum(sizes)],
    )


def solution(mesh):
    placed = (P("dp", "tm", "space", None, None), P("dp", "tm", "space", None, None), P(), P(), P())
    return jax.shard_map(
        per_device,
        mesh=mesh,
        in_specs=placed,
        out_specs=(
            P("dp", "tm", "space", None, None),
            P("space", ("dp", "tm")),
            P("space", ("dp", "tm")),
            P("space", ("dp", "tm")),
        ),
        check_vma=False,
    )
```

time: 69.2 us -> 53.7 us (0.78)
  Pallas kernels: 24.1 us -> 45.3 us
  starting transfers between devices: 18.6 us -> 0 us
  matrix products: 10 us -> 0 us
  waiting for transfers between devices: 5.24 us -> 0 us
  other arithmetic: 1.36 us -> 0 us
  local copies, waits for them, and re-layouts: 8.32 us -> 7.38 us
    pallas_call x1, Pallas kernels: 24.1 us -> 45.3 us  [per_device(): pl.pallas_call(functools.partial(block_kernel, groups, bands, cols, scale...]
    ppermute x7 -> x0, starting transfers between devices: 18.6 us -> none  [the longest x2 8.74 us: padded_2(): lax.ppermute(tail, axis, [(i, (i + 1) % count) for i in range(ends)])]
    dot_general x13 -> x0, matrix products: 10 us -> none  [the longest x7 3.3 us: contract(): lax.dot_general(merge_cells(left), merge_cells(right), (((0,), (0,)), (()...]
    ppermute x7 -> x0, waiting for transfers between devices: 5.24 us -> none  [the longest x2 4.99 us: padded_2(): lax.ppermute(head, axis, [((i + 1) % count, i) for i in range(ends)])]
    unnamed x21 -> x11, local copies, waits for them, and re-layouts: 2.03 us -> 6.04 us
    transpose x2 -> x0, local copies, waits for them, and re-layouts: 2.74 us -> none  [flip_blocks(): weight.reshape(taps, chans, chans).transpose(0, 2, 1)]
    slice x5 -> x2, local copies, waits for them, and re-layouts: 3.12 us -> 1.34 us  [the longest x1 0.69 us: per_device(): reduced[:, sizes[0] + sizes[1]:sum(sizes)]]
    concatenate x5 -> x0, other arithmetic: 0.92 us -> none  [the longest x2 0.74 us: padded_2(): jnp.concatenate([lax.ppermute(tail, axis, [(i, (i + 1) % count) for i in...]
  transfers between devices with their start and end apart: 7 -> 0, of which waited for: 3 -> 0; matrix products, arithmetic and copies ran while one was open for 24% -> 0% of each run, Pallas kernels for 0% -> 0%
where the time goes in v2:
time: 53.7 us; the launch traced here: 53.4 us
  Pallas kernels  45.3 us (84%)
  local copies, waits for them, and re-layouts  7.38 us (14%)
  between operations  0.65 us (1%)
    pallas_call x1, Pallas kernels, per_device(): pl.pallas_call(functools.partial(block_kernel, groups, bands, cols, scale...  45.3 us
    unnamed x11, local copies, waits for them, and re-layouts  6.04 us

profile of v2, /device:TPU:0, one launch (start us, length us, event | category | flops | bytes accessed | tf_op | source)
XLA Modules:
  0.0 53.4 jit_solution(11593213213142159449)
XLA Ops:
  0.6 0.0 copy-start
  0.6 1.3 %copy-done = bf16[2304,256]{1,0:T(8,128)(2,1)S(1)} copy-done((bf16[2304,256]{1,0:T(8,128)(2,1)S(1)}, bf16[2304,256]{1,0:T(8,128)(2,1)}, u32[]{:S(2)}) %copy-start) | copy-done | bytes 1179672
  1.9 0.0 copy-start.1
  1.9 1.0 %copy-done.1 = bf16[1,2,16,32,256]{4,3,2,1,0:T(8,128)(2,1)S(1)} copy-done((bf16[1,2,16,32,256]{4,3,2,1,0:T(8,128)(2,1)S(1)}, bf16[1,2,16,32,256]{4,3,2,1,0:T(8,128)(2,1)}, u32[]{:S(2)}) %copy-start.1) | copy-done | bytes 524312
  2.9 0.0 copy-start.2
  2.9 1.0 %copy-done.2 = bf16[768,256]{1,0:T(8,128)(2,1)S(1)} copy-done((bf16[768,256]{1,0:T(8,128)(2,1)S(1)}, bf16[768,256]{1,0:T(8,128)(2,1)}, u32[]{:S(2)}) %copy-start.2) | copy-done | bytes 393240
  3.9 0.0 copy-start.3
  3.9 1.0 %copy-done.3 = bf16[768,256]{1,0:T(8,128)(2,1)S(1)} copy-done((bf16[768,256]{1,0:T(8,128)(2,1)S(1)}, bf16[768,256]{1,0:T(8,128)(2,1)}, u32[]{:S(2)}) %copy-start.3) | copy-done | bytes 393240
  4.9 0.0 copy-start.4
  4.9 0.9 %copy-done.4 = bf16[1,1,16,32,256]{4,3,2,1,0:T(8,128)(2,1)S(1)} copy-done((bf16[1,1,16,32,256]{4,3,2,1,0:T(8,128)(2,1)S(1)}, bf16[1,1,16,32,256]{4,3,2,1,0:T(8,128)(2,1)}, u32[]{:S(2)}) %copy-start.4) | copy-done | bytes 262168
  5.9 45.3 %shard_map.84 = (bf16[2,512,256]{2,1,0:T(8,128)(2,1)S(1)}, f32[64,512]{1,0:T(8,128)S(1)}) custom-call(bf16[2,512,256]{2,1,0:T(8,128)(2,1)S(1)} %bitcast.4, bf16[512,256]{1,0:T(8,128)(2,1)S(1)} %bitcast.5, bf16[2304,256]{1,0:T(8,128)(2,1)S(1)} %copy-done, bf16[768,256]{1,0:T(8,128)(2,1)S(1)} %copy-done.2, bf16[768,256]{1,0:T(8,128)(2,1)S(1)} %copy-done.3), custom_call_target="tpu_custom_call" | custom-call | tf_op jit(solution)/shard_map/pallas_call | solution.py:373
  51.2 0.7 %fusion = (f32[64,96]{1,0:T(8,128)}, f32[64,96]{1,0:T(8,128)}) fusion(f32[64,512]{1,0:T(8,128)S(1)} %get-tuple-element.7), kind=kLoop, calls=%fused_computation | loop fusion | bytes 98304 | tf_op jit(solution)/shard_map/slice | solution.py:422
  51.9 0.6 %slice.9 = f32[64,288]{1,0:T(8,128)} slice(f32[64,512]{1,0:T(8,128)S(1)} %get-tuple-element.7), slice={[0:64], [0:288]} | slice | bytes 147456 | tf_op jit(solution)/shard_map/slice | solution.py:420
  52.6 0.8 %copy.10 = bf16[1,2,16,32,256]{4,3,2,1,0:T(8,128)(2,1)} copy(bf16[1,2,16,32,256]{4,3,2,1,0:T(8,128)(2,1)S(1)} %bitcast.3) | data formatting | bytes 1048576
Async XLA Ops:
  0.6 1.3 %copy-start = (bf16[2304,256]{1,0:T(8,128)(2,1)S(1)}, bf16[2304,256]{1,0:T(8,128)(2,1)}, u32[]{:S(2)}) copy-start(bf16[2304,256]{1,0:T(8,128)(2,1)} %ws_ref.1) | copy-start | bytes 3538948
  1.9 1.0 %copy-start.1 = (bf16[1,2,16,32,256]{4,3,2,1,0:T(8,128)(2,1)S(1)}, bf16[1,2,16,32,256]{4,3,2,1,0:T(8,128)(2,1)}, u32[]{:S(2)}) copy-start(bf16[1,2,16,32,256]{4,3,2,1,0:T(8,128)(2,1)} %param.5) | copy-start | bytes 1572868
  2.9 1.0 %copy-start.2 = (bf16[768,256]{1,0:T(8,128)(2,1)S(1)}, bf16[768,256]{1,0:T(8,128)(2,1)}, u32[]{:S(2)}) copy-start(bf16[768,256]{1,0:T(8,128)(2,1)} %wt_ref.1) | copy-start | bytes 1179652
  3.9 1.0 %copy-start.3 = (bf16[768,256]{1,0:T(8,128)(2,1)S(1)}, bf16[768,256]{1,0:T(8,128)(2,1)}, u32[]{:S(2)}) copy-start(bf16[768,256]{1,0:T(8,128)(2,1)} %wd_ref.1) | copy-start | bytes 1179652
  4.9 0.9 %copy-start.4 = (bf16[1,1,16,32,256]{4,3,2,1,0:T(8,128)(2,1)S(1)}, bf16[1,1,16,32,256]{4,3,2,1,0:T(8,128)(2,1)}, u32[]{:S(2)}) copy-start(bf16[1,1,16,32,256]{4,3,2,1,0:T(8,128)(2,1)} %param.6) | copy-start | bytes 786436

commit v3 on v2

v3 whole, which is shorter than its diff:
```python
import functools
import math

import jax
import jax.numpy as jnp
from jax import lax
from jax.experimental import pallas as pl
from jax.experimental.pallas import tpu as pltpu
from jax.sharding import PartitionSpec as P

F32 = jnp.float32
BF16 = jnp.bfloat16


def round_up(size, step):
    return (size + step - 1) // step * step


def dot_nn(left, right):
    return jnp.dot(left, right, preferred_element_type=F32)


def dot_nt(left, right):
    return lax.dot_general(left, right, (((1,), (1,)), ((), ())), preferred_element_type=F32)


def dot_tn(left, right):
    return lax.dot_general(left, right, (((0,), (0,)), ((), ())), preferred_element_type=F32)


def block_kernel(
    groups,
    bands,
    cols,
    scale,
    x_far,
    go_far,
    ws_far,
    wt_far,
    wd_far,
    latent_ref,
    out_ref,
    out_late,
    x_ref,
    go_ref,
    ws_ref,
    wt_ref,
    wd_ref,
    load_sem,
    x_pad,
    x_shift,
    a_pad,
    a_shift,
    pre,
    hid,
    ahead,
    dy,
    parts_0,
    parts_1,
    outgoing_0,
    outgoing_1,
    from_core_0,
    from_core_1,
    mid_0,
    mid_1,
    from_group_0,
    from_group_1,
    total_0,
    total_1,
    turned_0,
    turned_1,
    turned_wide_0,
    turned_wide_1,
    from_band_0,
    from_band_1,
    edge_send,
    edge_recv,
    core_send,
    core_recv,
    group_send,
    group_recv,
    band_send,
    band_recv,
):
    core = lax.axis_index("dp")
    group = lax.axis_index("tm")
    band = lax.axis_index("space")
    chans = x_ref.shape[2]
    cells = x_ref.shape[1]
    share = (9 * chans // (2 * groups), 3 * chans // (2 * groups), 3 * chans // (2 * groups))
    first = (0, 0, share[1])
    phase = (0, 1, 1)
    loads = [
        pltpu.make_async_copy(src, dst, load_sem.at[n])
        for n, (src, dst) in enumerate(
            (
                (x_far, x_ref),
                (ws_far, ws_ref),
                (go_far, go_ref),
                (wd_far, wd_ref),
                (wt_far, wt_ref),
            )
        )
    ]
    for load in loads:
        load.start()

    def at(d, t, s):
        return dict(device_id=(d, t, s), device_id_type=pl.DeviceIdType.MESH)

    barrier = pltpu.get_barrier_semaphore()
    pl.semaphore_signal(barrier, inc=1, **at(1 - core, group, band))
    for i in range(groups - 1):
        pl.semaphore_signal(barrier, inc=1, **at(core, lax.rem(group + 1 + i, groups), band))
    for i in range(bands - 1):
        pl.semaphore_signal(barrier, inc=1, **at(core, group, lax.rem(band + 1 + i, bands)))
    pl.semaphore_wait(barrier, groups + bands - 1)

    def make(n, src, dst, where):
        return pltpu.make_async_remote_copy(
            src_ref=src,
            dst_ref=dst,
            send_sem=edge_send.at[n],
            recv_sem=edge_recv.at[n],
            **where,
        )

    below = lax.rem(band + 1, bands)
    above = lax.rem(band + bands - 1, bands)
    before = lax.rem(group + groups - 1, groups)
    before2 = lax.rem(group + groups - 2, groups)
    after = lax.rem(group + 1, groups)
    low = pl.ds(0, cols)
    high = pl.ds(cells + cols, cols)
    moves = (
        (
            lambda: make(0, x_far.at[:, pl.ds(cells - cols, cols)], x_pad.at[:, low], at(core, group, below)),
            band < bands - 1,
            band > 0,
        ),
        (
            lambda: make(1, x_far.at[:, pl.ds(0, cols)], x_pad.at[:, high], at(core, group, above)),
            band > 0,
            band < bands - 1,
        ),
        (
            lambda: make(2, go_far, ahead.at[0], at(core, before, band)),
            group > 0,
            group < groups - 1,
        ),
        (
            lambda: make(3, go_far, ahead.at[1], at(core, before2, band)),
            group > 1,
            group < groups - 2,
        ),
        (
            lambda: make(4, a_pad.at[:, pl.ds(cells, cols)], a_pad.at[:, low], at(core, group, below)),
            band < bands - 1,
            band > 0,
        ),
        (
            lambda: make(5, a_pad.at[:, pl.ds(cols, cols)], a_pad.at[:, high], at(core, group, above)),
            band > 0,
            band < bands - 1,
        ),
    )

    def start(n):
        @pl.when(moves[n][1])
        def _():
            moves[n][0]().start()

    def arrive(n):
        @pl.when(moves[n][2])
        def _():
            moves[n][0]().wait_recv()

    def sent(n):
        @pl.when(moves[n][1])
        def _():
            moves[n][0]().wait_send()

    for n in range(4):
        start(n)

    edge_zero = jnp.zeros((2, cols, chans), BF16)

    @pl.when(band == 0)
    def _():
        x_pad[:, 0:cols] = edge_zero
        a_pad[:, 0:cols] = edge_zero

    @pl.when(band == bands - 1)
    def _():
        x_pad[:, cells + cols : cells + 2 * cols] = edge_zero
        a_pad[:, cells + cols : cells + 2 * cols] = edge_zero

    @pl.when(group == groups - 1)
    def _():
        ahead[0] = jnp.zeros((cells, chans), BF16)

    @pl.when(group >= groups - 2)
    def _():
        ahead[1] = jnp.zeros((cells, chans), BF16)

    def shift(source, target, order):
        length = cells + 2 * cols
        place = lax.rem(lax.broadcasted_iota(jnp.int32, (length, chans), 0), cols)
        for f in range(2):
            plain = source[f]
            wide = plain.astype(F32)
            left = jnp.where(place == 0, 0.0, pltpu.roll(wide, 1, 0)).astype(BF16)
            right = jnp.where(place == cols - 1, 0.0, pltpu.roll(wide, length - 1, 0)).astype(BF16)
            values = (left, plain, right)
            for j in range(3):
                target[f, :, j * chans : (j + 1) * chans] = values[order[j]]

    loads[0].wait()
    x_pad[:, cols : cells + cols] = x_ref[...]
    arrive(0)
    arrive(1)
    shift(x_pad, x_shift, (0, 1, 2))
    loads[1].wait()
    for f in range(2):
        acc = jnp.zeros((cells, chans), F32)
        for i in range(3):
            acc += dot_nn(
                x_shift[f, i * cols : i * cols + cells, :],
                ws_ref[3 * i * chans : 3 * (i + 1) * chans, :],
            )
        pre[f] = acc
        hid[f] = (acc / (1.0 + jnp.exp(-acc))).astype(BF16)
    arrive(2)
    arrive(3)
    for load in loads[2:]:
        load.wait()

    def down(k):
        return wd_ref[k * chans : (k + 1) * chans, :]

    def temporal(k):
        return wt_ref[k * chans : (k + 1) * chans, :]

    dy[0] = (dot_nt(go_ref[...], down(2)) + dot_nt(ahead[0], down(0))).astype(BF16)
    dy[1] = dot_nt(ahead[0], down(1)).astype(BF16)
    dy[2] = (dot_nt(ahead[0], down(2)) + dot_nt(ahead[1], down(0))).astype(BF16)
    dy[3] = dot_nt(ahead[1], down(1)).astype(BF16)
    both = (
        (parts_0, outgoing_0, from_core_0, mid_0, from_group_0, total_0),
        (parts_1, outgoing_1, from_core_1, mid_1, from_group_1, total_1),
    )

    def put(kind, begin, values):
        done = 0
        size = values.shape[0]
        while done < size:
            spot = begin + done
            owner, inner = spot // share[kind], spot % share[kind]
            count = min(share[kind] - inner, size - done)
            offset = first[kind] + inner
            both[phase[kind]][0][owner // groups, owner % groups, offset : offset + count, :] = values[
                done : done + count
            ]
            done += count

    for held, used in ((parts_0, share[0]), (parts_1, share[1] + share[2])):
        if held.shape[2] > used:
            for d in range(2):
                for t in range(groups):
                    held[d, t, used:, :] = jnp.zeros((held.shape[2] - used, chans), F32)

    core_copies = ([], [])
    group_copies = ([], [])
    band_copies = ([], [])

    def give_core(p):
        parts, outgoing, from_core = both[p][:3]
        for i in range(groups):
            target = lax.rem(group + 1 + i, groups)
            outgoing[i] = parts[1 - core, target].astype(BF16)
            copy = pltpu.make_async_remote_copy(
                src_ref=outgoing.at[i],
                dst_ref=from_core.at[i],
                send_sem=core_send.at[p, i],
                recv_sem=core_recv.at[p, i],
                **at(1 - core, group, band),
            )
            copy.start()
            core_copies[p].append(copy)

    def give_group(p):
        parts, _, from_core, mid, from_group, total = both[p]
        rows = parts.shape[2]
        for i in range(groups):
            target = lax.rem(group + 1 + i, groups)
            core_copies[p][i].wait_recv()
            summed = parts[core, target] + from_core[i].astype(F32)
            if i == groups - 1:
                total[0:rows, :] = summed
            else:
                mid[i] = summed.astype(BF16)
                copy = pltpu.make_async_remote_copy(
                    src_ref=mid.at[i],
                    dst_ref=from_group.at[i],
                    send_sem=group_send.at[p, i],
                    recv_sem=group_recv.at[p, i],
                    **at(core, target, band),
                )
                copy.start()
                group_copies[p].append(copy)
        if total.shape[0] > rows:
            total[rows:, :] = jnp.zeros((total.shape[0] - rows, chans), F32)

    last = (
        (turned_0, turned_wide_0, from_band_0, out_ref),
        (turned_1, turned_wide_1, from_band_1, out_late),
    )

    def give_band(p):
        from_group, total = both[p][4:]
        turned, turned_wide, from_band, _ = last[p]
        rows = from_group.shape[1]
        for i in range(groups - 1):
            group_copies[p][i].wait_recv()
            total[0:rows, :] += from_group[i].astype(F32)
        flat = (total[...] * scale).T.reshape(turned.shape)
        turned_wide[...] = flat
        turned[...] = flat.astype(BF16)
        for i in range(bands - 1):
            target = lax.rem(band + 1 + i, bands)
            copy = pltpu.make_async_remote_copy(
                src_ref=turned.at[target],
                dst_ref=from_band.at[i],
                send_sem=band_send.at[p, i],
                recv_sem=band_recv.at[p, i],
                **at(core, group, target),
            )
            copy.start()
            band_copies[p].append(copy)

    def finish(p):
        _, turned_wide, from_band, result_ref = last[p]
        result = turned_wide[band]
        for i in range(bands - 1):
            band_copies[p][i].wait_recv()
            result += from_band[i].astype(F32)
        result_ref[...] = result

    for k in range(3):
        put(1, k * chans, dot_tn(hid[0], dy[2 - k]) + dot_tn(hid[1], dy[3 - k]))
    pairs = (
        dot_tn(hid[0], ahead[1]),
        dot_tn(hid[1], ahead[1]),
        dot_tn(hid[0], ahead[0]),
        dot_tn(hid[1], ahead[0]),
        dot_tn(hid[0], go_ref[...]),
    )
    coarse = [pair.astype(BF16) for pair in pairs]
    fine = [(pair - part.astype(F32)).astype(BF16) for pair, part in zip(pairs, coarse)]
    direct = (
        dot_tn(x_ref[0], ahead[0]),
        dot_tn(x_ref[1], ahead[0]),
        dot_tn(x_ref[0], go_ref[...]),
    )
    for k in range(3):
        acc = direct[k]
        for n in range(3):
            acc += dot_tn(temporal(n), coarse[k + n]) + dot_tn(temporal(n), fine[k + n])
        put(2, k * chans, acc)
    give_core(1)
    for f in range(2):
        back = jnp.zeros((cells, chans), F32)
        for k in range(3):
            back += dot_nt(dy[f + 2 - k], temporal(k))
        value = pre[f]
        gate = 1.0 / (1.0 + jnp.exp(-value))
        a_pad[f, cols : cells + cols] = (back * gate * (1.0 + value * (1.0 - gate))).astype(BF16)
    start(4)
    start(5)

    give_group(1)
    for i in range(3):
        for j in range(3):
            acc = jnp.zeros((chans, chans), F32)
            for f in range(2):
                acc += dot_tn(
                    x_shift[f, i * cols : i * cols + cells, j * chans : (j + 1) * chans],
                    a_pad[f, cols : cells + cols, :],
                )
            put(0, (3 * i + j) * chans, acc)
    give_core(0)
    give_band(1)
    give_group(0)
    arrive(4)
    arrive(5)
    shift(a_pad, a_shift, (2, 1, 0))
    for f in range(2):
        acc = dy[f].astype(F32)
        for i in range(3):
            for j in range(3):
                tap = 3 * i + j
                acc += dot_nt(
                    a_shift[f, (2 - i) * cols : (2 - i) * cols + cells, j * chans : (j + 1) * chans],
                    ws_ref[tap * chans : (tap + 1) * chans, :],
                )
        latent_ref[f] = acc.astype(BF16)

    give_band(0)
    finish(1)
    finish(0)
    for n in range(6):
        sent(n)
    for p in range(2):
        for copy in core_copies[p] + group_copies[p] + band_copies[p]:
            copy.wait_send()


def per_device(clip_latent, grad_out, w_spatial, w_temporal, w_down):
    clips, frames, height, cols, chans = clip_latent.shape
    groups = lax.axis_size("tm")
    bands = lax.axis_size("space")
    assert clips == 1 and frames == 2 and grad_out.shape[1] == 1 and lax.axis_size("dp") == 2
    count = clips * frames * height * cols * 2 * groups * bands
    scale = 1.0 / math.sqrt(count)
    cells = height * cols
    padded = cells + 2 * cols
    sizes = (9 * chans // (2 * groups), 3 * chans // (2 * groups), 3 * chans // (2 * groups))
    rows = (round_up(sizes[0], 16), round_up(sizes[1] + sizes[2], 16))
    wide = tuple(round_up(size, 128) for size in rows)
    share = chans // bands
    dma = pltpu.SemaphoreType.DMA
    vmem = pl.BlockSpec(memory_space=pltpu.VMEM)
    latent, spatial, others = pl.pallas_call(
        functools.partial(block_kernel, groups, bands, cols, scale),
        out_shape=(
            jax.ShapeDtypeStruct((2, cells, chans), BF16),
            jax.ShapeDtypeStruct((share, wide[0]), F32),
            jax.ShapeDtypeStruct((share, wide[1]), F32),
        ),
        in_specs=[pl.BlockSpec(memory_space=pl.ANY)] * 5,
        out_specs=(vmem, vmem, vmem),
        scratch_shapes=[
            pltpu.VMEM((2, cells, chans), BF16),
            pltpu.VMEM((cells, chans), BF16),
            pltpu.VMEM(w_spatial.shape, BF16),
            pltpu.VMEM(w_temporal.shape, BF16),
            pltpu.VMEM(w_down.shape, BF16),
            dma((5,)),
            pltpu.VMEM((2, padded, chans), BF16),
            pltpu.VMEM((2, padded, 3 * chans), BF16),
            pltpu.VMEM((2, padded, chans), BF16),
            pltpu.VMEM((2, padded, 3 * chans), BF16),
            pltpu.VMEM((2, cells, chans), F32),
            pltpu.VMEM((2, cells, chans), BF16),
            pltpu.VMEM((2, cells, chans), BF16),
            pltpu.VMEM((4, cells, chans), BF16),
            pltpu.VMEM((2, groups, rows[0], chans), F32),
            pltpu.VMEM((2, groups, rows[1], chans), F32),
            pltpu.VMEM((groups, rows[0], chans), BF16),
            pltpu.VMEM((groups, rows[1], chans), BF16),
            pltpu.VMEM((groups, rows[0], chans), BF16),
            pltpu.VMEM((groups, rows[1], chans), BF16),
            pltpu.VMEM((groups - 1, rows[0], chans), BF16),
            pltpu.VMEM((groups - 1, rows[1], chans), BF16),
            pltpu.VMEM((groups - 1, rows[0], chans), BF16),
            pltpu.VMEM((groups - 1, rows[1], chans), BF16),
            pltpu.VMEM((wide[0], chans), F32),
            pltpu.VMEM((wide[1], chans), F32),
            pltpu.VMEM((bands, share, wide[0]), BF16),
            pltpu.VMEM((bands, share, wide[1]), BF16),
            pltpu.VMEM((bands, share, wide[0]), F32),
            pltpu.VMEM((bands, share, wide[1]), F32),
            pltpu.VMEM((bands - 1, share, wide[0]), BF16),
            pltpu.VMEM((bands - 1, share, wide[1]), BF16),
            dma((6,)),
            dma((6,)),
            dma((2, groups)),
            dma((2, groups)),
            dma((2, groups - 1)),
            dma((2, groups - 1)),
            dma((2, bands - 1)),
            dma((2, bands - 1)),
        ],
        compiler_params=pltpu.CompilerParams(
            collective_id=0, has_side_effects=True, vmem_limit_bytes=58 * 1024 * 1024
        ),
    )(
        clip_latent.reshape(2, cells, chans),
        grad_out.reshape(cells, chans),
        w_spatial,
        w_temporal,
        w_down,
    )
    return (
        latent.reshape(clip_latent.shape),
        spatial[:, : sizes[0]],
        others[:, : sizes[1]],
        others[:, sizes[1] : sizes[1] + sizes[2]],
    )


def solution(mesh):
    placed = (P("dp", "tm", "space", None, None), P("dp", "tm", "space", None, None), P(), P(), P())
    return jax.shard_map(
        per_device,
        mesh=mesh,
        in_specs=placed,
        out_specs=(
            P("dp", "tm", "space", None, None),
            P("space", ("dp", "tm")),
            P("space", ("dp", "tm")),
            P("space", ("dp", "tm")),
        ),
        check_vma=False,
    )
```

time: 53.7 us -> 46.9 us (0.87)
  local copies, waits for them, and re-layouts: 7.38 us -> 4.08 us
  Pallas kernels: 45.3 us -> 42 us
    unnamed x11 -> x4, local copies, waits for them, and re-layouts: 6.04 us -> 2.51 us
    pallas_call x1, Pallas kernels: 45.3 us -> 42 us  [per_device(): pl.pallas_call(functools.partial(block_kernel, groups, bands, cols, scale...]
    slice x2 -> x1, local copies, waits for them, and re-layouts: 1.34 us -> 1.57 us  [per_device(): others[:, sizes[1]:sizes[1] + sizes[2]]]
where the time goes in v3:
time: 46.9 us; the launch traced here: 46.7 us
  Pallas kernels  42 us (90%)
  local copies, waits for them, and re-layouts  4.08 us (9%)
  between operations  0.65 us (1%)
    pallas_call x1, Pallas kernels, per_device(): pl.pallas_call(functools.partial(block_kernel, groups, bands, cols, scale...  42 us
    unnamed x4, local copies, waits for them, and re-layouts  2.51 us
    slice x1, local copies, waits for them, and re-layouts, per_device(): others[:, sizes[1]:sizes[1] + sizes[2]]  1.57 us

profile of v3, /device:TPU:0, one launch (start us, length us, event | category | flops | bytes accessed | tf_op | source)
XLA Modules:
  0.0 46.7 jit_solution(12199652211540519168)
XLA Ops:
  0.6 42.0 %shard_map.84 = (bf16[2,512,256]{2,1,0:T(8,128)(2,1)}, f32[64,384]{1,0:T(8,128)}, f32[64,256]{1,0:T(8,128)}) custom-call(bf16[2,512,256]{2,1,0:T(8,128)(2,1)} %bitcast.5, bf16[512,256]{1,0:T(8,128)(2,1)} %bitcast.6, bf16[2304,256]{1,0:T(8,128)(2,1)} %ws_far.1, bf16[768,256]{1,0:T(8,128)(2,1)} %wt_far.1, bf16[768,256]{1,0:T(8,128)(2,1)} %wd_far.1), custom_call_target="tpu_custom_call" | custom-call | tf_op jit(solution)/shard_map/pallas_call | solution.py:433
  42.7 0.0 copy-start
  42.7 1.6 %fusion = (f32[64,96]{1,0:T(8,128)}, f32[64,96]{1,0:T(8,128)}) fusion(f32[64,256]{1,0:T(8,128)} %get-tuple-element.9), kind=kLoop, calls=%fused_computation | loop fusion | bytes 98304 | tf_op jit(solution)/shard_map/slice | solution.py:498
  44.2 1.9 %copy.11 = bf16[1,2,16,32,256]{4,3,2,1,0:T(8,128)(2,1)} copy(bf16[1,2,16,32,256]{4,3,2,1,0:T(8,128)(2,1)} %bitcast.4) | data formatting | bytes 1048576
  46.1 0.0 copy-done
  46.1 0.6 %copy.12 = f32[64,288]{1,0:T(8,128)} copy(f32[64,288]{1,0:T(8,128)S(1)} %bitcast.7) | data formatting | bytes 147456
Async XLA Ops:
  42.7 3.5 %copy-start = (f32[64,384]{1,0:T(8,128)S(1)}, f32[64,384]{1,0:T(8,128)}, u32[]{:S(2)}) copy-start(f32[64,384]{1,0:T(8,128)} %get-tuple-element.8) | copy-start | bytes 294916

commit v4 on v3

--- a/solution.py
+++ b/solution.py
@@ -40,7 +40,8 @@
     wd_far,
     latent_ref,
     out_ref,
-    out_late,
+    out_temporal,
+    out_down,
     x_ref,
     go_ref,
     ws_ref,
@@ -231,7 +232,6 @@
         pre[f] = acc
         hid[f] = (acc / (1.0 + jnp.exp(-acc))).astype(BF16)
     arrive(2)
-    arrive(3)
     for load in loads[2:]:
         load.wait()
 
@@ -243,8 +243,6 @@
 
     dy[0] = (dot_nt(go_ref[...], down(2)) + dot_nt(ahead[0], down(0))).astype(BF16)
     dy[1] = dot_nt(ahead[0], down(1)).astype(BF16)
-    dy[2] = (dot_nt(ahead[0], down(2)) + dot_nt(ahead[1], down(0))).astype(BF16)
-    dy[3] = dot_nt(ahead[1], down(1)).astype(BF16)
     both = (
         (parts_0, outgoing_0, from_core_0, mid_0, from_group_0, total_0),
         (parts_1, outgoing_1, from_core_1, mid_1, from_group_1, total_1),
@@ -312,8 +310,8 @@
             total[rows:, :] = jnp.zeros((total.shape[0] - rows, chans), F32)
 
     last = (
-        (turned_0, turned_wide_0, from_band_0, out_ref),
-        (turned_1, turned_wide_1, from_band_1, out_late),
+        (turned_0, turned_wide_0, from_band_0, ((out_ref, 0, share[0]),)),
+        (turned_1, turned_wide_1, from_band_1, ((out_temporal, 0, share[1]), (out_down, share[1], share[2]))),
     )
 
     def give_band(p):
@@ -339,29 +337,33 @@
             band_copies[p].append(copy)
 
     def finish(p):
-        _, turned_wide, from_band, result_ref = last[p]
+        _, turned_wide, from_band, results = last[p]
         result = turned_wide[band]
         for i in range(bands - 1):
             band_copies[p][i].wait_recv()
             result += from_band[i].astype(F32)
-        result_ref[...] = result
-
-    for k in range(3):
-        put(1, k * chans, dot_tn(hid[0], dy[2 - k]) + dot_tn(hid[1], dy[3 - k]))
-    pairs = (
-        dot_tn(hid[0], ahead[1]),
-        dot_tn(hid[1], ahead[1]),
+        for result_ref, begin, size in results:
+            result_ref[...] = result[:, begin : begin + size]
+
+    put(1, 2 * chans, dot_tn(hid[0], dy[0]) + dot_tn(hid[1], dy[1]))
+    near_pairs = (
         dot_tn(hid[0], ahead[0]),
         dot_tn(hid[1], ahead[0]),
         dot_tn(hid[0], go_ref[...]),
     )
-    coarse = [pair.astype(BF16) for pair in pairs]
-    fine = [(pair - part.astype(F32)).astype(BF16) for pair, part in zip(pairs, coarse)]
     direct = (
         dot_tn(x_ref[0], ahead[0]),
         dot_tn(x_ref[1], ahead[0]),
         dot_tn(x_ref[0], go_ref[...]),
     )
+    arrive(3)
+    dy[2] = (dot_nt(ahead[0], down(2)) + dot_nt(ahead[1], down(0))).astype(BF16)
+    dy[3] = dot_nt(ahead[1], down(1)).astype(BF16)
+    for k in range(2):
+        put(1, k * chans, dot_tn(hid[0], dy[2 - k]) + dot_tn(hid[1], dy[3 - k]))
+    pairs = (dot_tn(hid[0], ahead[1]), dot_tn(hid[1], ahead[1])) + near_pairs
+    coarse = [pair.astype(BF16) for pair in pairs]
+    fine = [(pair - part.astype(F32)).astype(BF16) for pair, part in zip(pairs, coarse)]
     for k in range(3):
         acc = direct[k]
         for n in range(3):
@@ -430,15 +432,16 @@
     share = chans // bands
     dma = pltpu.SemaphoreType.DMA
     vmem = pl.BlockSpec(memory_space=pltpu.VMEM)
-    latent, spatial, others = pl.pallas_call(
+    latent, spatial, temporal, down = pl.pallas_call(
         functools.partial(block_kernel, groups, bands, cols, scale),
         out_shape=(
             jax.ShapeDtypeStruct((2, cells, chans), BF16),
-            jax.ShapeDtypeStruct((share, wide[0]), F32),
-            jax.ShapeDtypeStruct((share, wide[1]), F32),
-        ),
-        in_specs=[pl.BlockSpec(memory_space=pl.ANY)] * 5,
-        out_specs=(vmem, vmem, vmem),
+            jax.ShapeDtypeStruct((share, sizes[0]), F32),
+            jax.ShapeDtypeStruct((share, sizes[1]), F32),
+            jax.ShapeDtypeStruct((share, sizes[2]), F32),
+        ),
+        in_specs=[pl.BlockSpec(memory_space=pltpu.HBM)] * 5,
+        out_specs=(vmem, vmem, vmem, vmem),
         scratch_shapes=[
             pltpu.VMEM((2, cells, chans), BF16),
             pltpu.VMEM((cells, chans), BF16),
@@ -493,9 +496,9 @@
     )
     return (
         latent.reshape(clip_latent.shape),
-        spatial[:, : sizes[0]],
-        others[:, : sizes[1]],
-        others[:, sizes[1] : sizes[1] + sizes[2]],
+        spatial,
+        temporal,
+        down,
     )
 
 

time: 46.9 us -> 47.1 us (level)
  local copies, waits for them, and re-layouts: 4.08 us -> 4.66 us
    unnamed x4 -> x8, local copies, waits for them, and re-layouts: 2.51 us -> 4.66 us
    slice x1 -> x0, local copies, waits for them, and re-layouts: 1.57 us -> none  [per_device(): others[:, sizes[1]:sizes[1] + sizes[2]]]
where the time goes in v4:
time: 47.1 us; the launch traced here: 46.9 us
  Pallas kernels  41.6 us (88%)
  local copies, waits for them, and re-layouts  4.66 us (10%)
  between operations  0.66 us (1%)
    pallas_call x1, Pallas kernels, per_device(): pl.pallas_call(functools.partial(block_kernel, groups, bands, cols, scale...  41.6 us
    unnamed x8, local copies, waits for them, and re-layouts  4.66 us

profile of v4, /device:TPU:0, one launch (start us, length us, event | category | flops | bytes accessed | tf_op | source)
XLA Modules:
  0.0 46.9 jit_solution(12941081995698376059)
XLA Ops:
  0.6 41.6 %shard_map.84 = (bf16[2,512,256]{2,1,0:T(8,128)(2,1)}, f32[64,288]{1,0:T(8,128)}, f32[64,96]{1,0:T(8,128)}, f32[64,96]{1,0:T(8,128)}) custom-call(bf16[2,512,256]{2,1,0:T(8,128)(2,1)} %bitcast.4, bf16[512,256]{1,0:T(8,128)(2,1)} %bitcast.5, bf16[2304,256]{1,0:T(8,128)(2,1)} %ws_far.1, bf16[768,256]{1,0:T(8,128)(2,1)} %wt_far.1, bf16[768,256]{1,0:T(8,128)(2,1)} %wd_far.1), custom_call_target="tpu_custom_call" | custom-call | tf_op jit(solution)/shard_map/pallas_call | solution.py:435
  42.2 0.0 copy-start.1
  42.2 0.0 copy-start
  42.2 1.9 %copy.13 = bf16[1,2,16,32,256]{4,3,2,1,0:T(8,128)(2,1)} copy(bf16[1,2,16,32,256]{4,3,2,1,0:T(8,128)(2,1)} %bitcast.3) | data formatting | bytes 1048576
  44.1 1.5 %copy.14 = f32[64,288]{1,0:T(8,128)} copy(f32[64,288]{1,0:T(8,128)} %get-tuple-element.17) | data formatting | bytes 147456
  45.7 0.0 copy-done.1
  45.7 0.6 %copy.15 = f32[64,96]{1,0:T(8,128)} copy(f32[64,96]{1,0:T(8,128)S(1)} %copy-done.1) | data formatting | bytes 49152
  46.3 0.0 copy-done
  46.3 0.6 %copy.16 = f32[64,96]{1,0:T(8,128)} copy(f32[64,96]{1,0:T(8,128)S(1)} %copy-done) | data formatting | bytes 49152
Async XLA Ops:
  42.2 3.4 %copy-start.1 = (f32[64,96]{1,0:T(8,128)S(1)}, f32[64,96]{1,0:T(8,128)}, u32[]{:S(2)}) copy-start(f32[64,96]{1,0:T(8,128)} %get-tuple-element.18) | copy-start | bytes 73732
  42.2 4.0 %copy-start = (f32[64,96]{1,0:T(8,128)S(1)}, f32[64,96]{1,0:T(8,128)}, u32[]{:S(2)}) copy-start(f32[64,96]{1,0:T(8,128)} %get-tuple-element.19) | copy-start | bytes 73732
